TPU v7x, 256 devices: a whole 4x4x8 slice. The times are simulated.
256 devices in a mesh: ctx: 64 (over z, y, core), head: 4 (over x).
Axes of the slice: x: 4, y: 4, z: 8, core: 2. Of those that a mesh axis runs over, the one named last changes fastest.
Arguments:
- sec_q: bfloat16 [8192, 1536], P('ctx', 'head'), may hold values from -7 to 7
- sec_k: bfloat16 [8192, 1536], P('ctx', 'head'), may hold values from -6 to 6
- sec_v: bfloat16 [8192, 1536], P('ctx', 'head'), may hold values from -6 to 6
- hist_k: bfloat16 [2048, 1536], P('ctx', 'head'), may hold values from -6 to 6
- hist_v: bfloat16 [2048, 1536], P('ctx', 'head'), may hold values from -6 to 6
- frame_levels: int32 [64, 2], replicated, may hold values from 0 to 2, as said below
- frame_counts: int32 [64], replicated, may hold values from 1 to 2, as said below
- w_out: bfloat16 [1536, 3072], P('head'), may hold values from -0.15625 to 0.15625
- grad_out: bfloat16 [8192, 3072], P('ctx', 'head'), may hold values from -6 to 6
Outputs:
- out: bfloat16 [8192, 3072], P('ctx', 'head')
- grad_sec_q: bfloat16 [8192, 1536], P('ctx', 'head')
- grad_sec_k: bfloat16 [8192, 1536], P('ctx', 'head')
- grad_sec_v: bfloat16 [8192, 1536], P('ctx', 'head')
- grad_hist_k: bfloat16 [2048, 1536], P('ctx', 'head')
- grad_hist_v: bfloat16 [2048, 1536], P('ctx', 'head')
Inputs may be any that keep to these rules, and one draw needn't show every extreme that they name: `frame_levels`: only the first frame_counts[o] levels of owner o count; the tokens of one owner never exceed 32, and in every draw some owner has exactly 32. `frame_counts`: in every draw some owner has 2 frames.
All inputs are finite; a program needn't handle non-finite values.
Results may differ from a plain program's by a relative error of at most 0.033.
Values may be sent and summed in bfloat16 or wider, within the bound.
A program may use at most 192 MiB of HBM per device.

v0:
```python
import math

import jax
import jax.numpy as jnp
from jax import lax
from jax.sharding import PartitionSpec as P

HDIM = 128
FTOK = 16
FMAX = 2


NEG_FILL = -1e30


def contract_rows(left_side, right_side):
    return lax.dot_general(
        left_side, right_side, (((0,), (0,)), ((), ())), preferred_element_type=jnp.float32
    )


def contract_cols(left_side, right_side):
    return lax.dot_general(
        left_side, right_side, (((1,), (1,)), ((), ())), preferred_element_type=jnp.float32
    )


def head_slice(stacked, head_idx):
    return stacked[:, head_idx * HDIM : (head_idx + 1) * HDIM]


def owner_token_counts(frame_levels, frame_counts):
    frame_index = jnp.arange(FMAX, dtype=jnp.int32)[None, :]
    per_frame = jnp.where(
        frame_index < frame_counts[:, None], jnp.right_shift(jnp.int32(FTOK), 2 * frame_levels), 0
    )
    return jnp.sum(per_frame, axis=1)


def shards(sec_q, sec_k, sec_v, hist_k, hist_v, frame_levels, frame_counts, w_out, grad_out):
    score_scale = 1.0 / math.sqrt(HDIM)
    sec_rows = sec_q.shape[0]
    width_here = sec_q.shape[1]
    heads_here = width_here // HDIM
    capacity = hist_k.shape[0]
    owners = lax.axis_size("ctx")
    owner_tokens = owner_token_counts(frame_levels, frame_counts)
    slot_index = jnp.arange(capacity, dtype=jnp.int32)
    hist_valid = (slot_index[None, :] < owner_tokens[:, None]).reshape(owners * capacity)
    key_valid = jnp.concatenate([jnp.ones((owners * sec_rows,), dtype=bool), hist_valid])
    gathered = (
        lax.all_gather(sec_k, "ctx", axis=0, tiled=True),
        lax.all_gather(sec_v, "ctx", axis=0, tiled=True),
        lax.all_gather(hist_k, "ctx", axis=0, tiled=True),
        lax.all_gather(hist_v, "ctx", axis=0, tiled=True),
    )
    all_keys = jnp.concatenate([gathered[0], gathered[2]], axis=0)
    all_values = jnp.concatenate([gathered[1], gathered[3]], axis=0)
    d_attn = contract_cols(lax.all_gather(grad_out, "head", axis=1, tiled=True), w_out).astype(
        jnp.bfloat16
    )
    attn_parts = []
    grad_q_parts = []
    log_totals = []
    row_deltas = []
    prob_list = []
    dscore_list = []
    for head_idx in range(heads_here):
        query_h = head_slice(sec_q, head_idx)
        key_h = head_slice(all_keys, head_idx)
        value_h = head_slice(all_values, head_idx)
        dattn_h = head_slice(d_attn, head_idx)
        scores = contract_cols(query_h, key_h) * score_scale
        scores = jnp.where(key_valid[None, :], scores, NEG_FILL)
        row_top = jnp.max(scores, axis=1, keepdims=True)
        log_total = row_top + jnp.log(jnp.sum(jnp.exp(scores - row_top), axis=1, keepdims=True))
        prob_h = jnp.where(key_valid[None, :], jnp.exp(scores - log_total), 0.0).astype(
            jnp.bfloat16
        )
        attn_h = jnp.dot(prob_h, value_h, preferred_element_type=jnp.float32).astype(jnp.bfloat16)
        row_delta = jnp.sum(attn_h.astype(jnp.float32) * dattn_h.astype(jnp.float32), axis=1)
        dprobs = contract_cols(dattn_h, value_h)
        dscores = (prob_h.astype(jnp.float32) * (dprobs - row_delta[:, None])).astype(jnp.bfloat16)
        grad_query = (
            jnp.dot(dscores, key_h, preferred_element_type=jnp.float32) * score_scale
        ).astype(jnp.bfloat16)
        attn_parts.append(attn_h)
        grad_q_parts.append(grad_query)
        log_totals.append(log_total[:, 0])
        row_deltas.append(row_delta)
        prob_list.append(prob_h)
        dscore_list.append(dscores)
    attn = jnp.concatenate(attn_parts, axis=1)
    grad_sec_q = jnp.concatenate(grad_q_parts, axis=1)
    partial_out = jnp.dot(attn, w_out, preferred_element_type=jnp.float32)
    share_cols = partial_out.shape[1] // lax.axis_size("head")
    full_out = lax.psum(partial_out.astype(jnp.bfloat16), "head").astype(jnp.float32)
    out = lax.dynamic_slice_in_dim(
        full_out, lax.axis_index("head") * share_cols, share_cols, 1
    ).astype(jnp.bfloat16)
    all_logs, all_deltas = (
        lax.all_gather(jnp.stack(log_totals, 0), "ctx", axis=1, tiled=True),
        lax.all_gather(jnp.stack(row_deltas, 0), "ctx", axis=1, tiled=True),
    )
    own_keys = jnp.concatenate([sec_k, hist_k], axis=0)
    own_values = jnp.concatenate([sec_v, hist_v], axis=0)
    own_count = jnp.sum(
        jnp.where(jnp.arange(owners, dtype=jnp.int32) == lax.axis_index("ctx"), owner_tokens, 0)
    )
    own_valid = jnp.concatenate([jnp.ones((sec_rows,), dtype=bool), slot_index < own_count])
    query_piece = lax.all_gather(sec_q, "ctx", axis=0, tiled=True)
    dattn_piece = lax.all_gather(d_attn, "ctx", axis=0, tiled=True)
    key_parts = []
    value_parts = []
    for head_idx in range(heads_here):
        query_ph = head_slice(query_piece, head_idx)
        dattn_ph = head_slice(dattn_piece, head_idx)
        scores = contract_cols(query_ph, head_slice(own_keys, head_idx)) * score_scale
        prob_ph = jnp.where(
            own_valid[None, :], jnp.exp(scores - all_logs[head_idx][:, None]), 0.0
        ).astype(jnp.bfloat16)
        dprobs = contract_cols(dattn_ph, head_slice(own_values, head_idx))
        dscores = (prob_ph.astype(jnp.float32) * (dprobs - all_deltas[head_idx][:, None])).astype(
            jnp.bfloat16
        )
        key_parts.append(contract_rows(dscores, query_ph))
        value_parts.append(contract_rows(prob_ph, dattn_ph))
    key_sum = jnp.concatenate(key_parts, axis=1)
    value_sum = jnp.concatenate(value_parts, axis=1)
    grad_keys = (key_sum * score_scale).astype(jnp.bfloat16)
    grad_values = value_sum.astype(jnp.bfloat16)
    return (
        out,
        grad_sec_q,
        grad_keys[:sec_rows],
        grad_values[:sec_rows],
        grad_keys[sec_rows:],
        grad_values[sec_rows:],
    )


def solution(mesh):
    placed = (
        P("ctx", "head"),
        P("ctx", "head"),
        P("ctx", "head"),
        P("ctx", "head"),
        P("ctx", "head"),
        P(),
        P(),
        P("head", None),
        P("ctx", "head"),
    )
    return jax.shard_map(
        shards,
        mesh=mesh,
        in_specs=placed,
        out_specs=(
            P("ctx", "head"),
            P("ctx", "head"),
            P("ctx", "head"),
            P("ctx", "head"),
            P("ctx", "head"),
            P("ctx", "head"),
        ),
        check_vma=False,
    )
```

profile of v0, /device:TPU:1, one launch (start us, length us, event | category | flops | bytes accessed | tf_op | source)
XLA Modules:
  0.0 564.4 jit_solution(7435122135675121723)
XLA Ops:
  10.6 13.1 %all_gather.31 = bf16[128,3072]{1,0:T(8,128)(2,1)S(1)} all-gather(bf16[128,768]{1,0:T(8,128)(2,1)} %param.17), channel_id=1, replica_groups=mesh['ctx'=64,'head'=4] {'head'}, dimensions={1}, use_global_device_ids=true | all-gather | bytes 983040 | tf_op jit(solution)/shard_map/all_gather | solution.py:59
  30.8 65.4 %all-gather.7.cloned.1.call-done = bf16[8192,384]{1,0:T(8,128)(2,1)} async-done(((bf16[128,384]{1,0:T(8,128)(2,1)}), bf16[8192,384]{1,0:T(8,128)(2,1)}) %all-gather.7.cloned.1.call-update) | async-done | bytes 6291472 | tf_op jit(solution)/shard_map/all_gather | solution.py:52
  96.1 6.0 %constant_dynamic-update-slice_fusion.1 = bf16[10240,384]{1,0:T(8,128)(2,1)} fusion(bf16[8192,384]{1,0:T(8,128)(2,1)} %all-gather.7.cloned.1.call-done), kind=kLoop, calls=%fused_computation.123 | loop fusion | bytes 12582912
  102.2 70.3 %all-gather.9.cloned.1.call-done = bf16[2048,384]{1,0:T(8,128)(2,1)} async-done(((bf16[32,384]{1,0:T(8,128)(2,1)}), bf16[2048,384]{1,0:T(8,128)(2,1)}) %all-gather.9.cloned.1.call-update) | async-done | bytes 1572880 | tf_op jit(solution)/shard_map/all_gather | solution.py:54
  175.2 7.9 %fusion.140 = (f32[128]{0:T(128)S(1)}, f32[10240,128]{1,0:T(8,128)S(1)}) fusion(bf16[128,384]{1,0:T(8,128)(2,1)S(1)} %copy-done.6, bf16[10240,384]{1,0:T(8,128)(2,1)} %constant_dynamic-update-slice_fusion, pred[10240]{0:T(1024)(128)(4,1)S(1)} %concatenate.31), kind=kOutput, calls=%fused_computation.143 | convolution fusion | flops 339476352 | bytes 7907840 | tf_op jit(solution)/shard_map/dot_general | solution.py:23
  192.8 48.5 %all_gather.33 = f32[3,8192]{1,0:T(4,128)S(1)} all-gather(f32[3,128]{1,0:T(4,128)S(1)} %pad_maximum_fusion.3), channel_id=1, replica_groups=mesh['ctx'=64,'head'=4] {'ctx'}, dimensions={1}, use_global_device_ids=true | all-gather | bytes 99840 | tf_op jit(solution)/shard_map/all_gather | solution.py:102
  241.3 12.8 %all-gather.11.cloned.1.call-done = bf16[8192,384]{1,0:T(8,128)(2,1)} async-done(((bf16[128,384]{1,0:T(8,128)(2,1)}), bf16[8192,384]{1,0:T(8,128)(2,1)}) %all-gather.11.cloned.1.call-update) | async-done | bytes 6291472 | tf_op jit(solution)/shard_map/all_gather | solution.py:53
  254.0 6.0 %constant_dynamic-update-slice_fusion.3 = bf16[10240,384]{1,0:T(8,128)(2,1)} fusion(bf16[8192,384]{1,0:T(8,128)(2,1)} %all-gather.11.cloned.1.call-done), kind=kLoop, calls=%fused_computation.125 | loop fusion | bytes 12582912
  260.1 70.2 %all-gather.13.cloned.1.call-done = bf16[2048,384]{1,0:T(8,128)(2,1)} async-done(((bf16[32,384]{1,0:T(8,128)(2,1)}), bf16[2048,384]{1,0:T(8,128)(2,1)}) %all-gather.13.cloned.1.call-update) | async-done | bytes 1572880 | tf_op jit(solution)/shard_map/all_gather | solution.py:55
  333.1 8.2 %fusion.102 = bf16[128,128]{0,1:T(8,128)(2,1)S(1)} fusion(bf16[10240,384]{1,0:T(8,128)(2,1)} %constant_dynamic-update-slice_fusion.2, f32[10240,128]{1,0:T(8,128)} %copy-done.1, f32[128]{0:T(128)S(1)} %log_add_fusion, pred[10240]{0:T(1024)(128)(4,1)S(1)} %concatenate.31), kind=kOutput, calls=%fused_computation.94 | convolution fusion | flops 339492864 | bytes 7907840 | tf_op jit(solution)/shard_map/dot_general | solution.py:80
  341.4 8.5 %fusion.99 = bf16[128,128]{0,1:T(8,128)(2,1)S(1)} fusion(bf16[10240,384]{1,0:T(8,128)(2,1)} %constant_dynamic-update-slice_fusion.2, f32[10240,128]{1,0:T(8,128)S(1)} %bitcast.43, f32[128]{0:T(128)S(1)} %log_add_fusion.1, pred[10240]{0:T(1024)(128)(4,1)S(1)} %concatenate.31), kind=kOutput, calls=%fused_computation.93 | convolution fusion | flops 339492864 | bytes 7907840 | tf_op jit(solution)/shard_map/dot_general | solution.py:80
  349.9 8.4 %multiply_reduce_fusion.2 = (f32[128]{0:T(128)S(1)}, f32[128]{0:T(128)S(1)}, f32[128]{0:T(128)S(1)}, bf16[128,128]{0,1:T(8,128)(2,1)S(1)}) fusion(bf16[128,384]{0,1:T(8,128)(2,1)S(1)} %copy-done.5, bf16[128,128]{0,1:T(8,128)(2,1)S(1)} %fusion.99, bf16[128,128]{0,1:T(8,128)(2,1)S(1)} %fusion.102, ...), kind=kOutput, calls=%fused_computation.107 | convolution fusion | flops 339689088 | bytes 8073216 | tf_op jit(solution)/shard_map/dot_general | solution.py:80
  358.3 48.3 %all_gather.35 = f32[3,8192]{1,0:T(4,128)S(1)} all-gather(f32[3,128]{1,0:T(4,128)S(1)} %pad_maximum_fusion.4), channel_id=1, replica_groups=mesh['ctx'=64,'head'=4] {'ctx'}, dimensions={1}, use_global_device_ids=true | all-gather | bytes 99840 | tf_op jit(solution)/shard_map/all_gather | solution.py:103
  406.7 5.0 all-gather.15.cloned.1.call-done
  411.7 4.6 fusion.21
  422.3 6.7 %fusion.87 = bf16[128,128]{0,1:T(8,128)(2,1)S(1)} fusion(bf16[10240,384]{1,0:T(8,128)(2,1)} %constant_dynamic-update-slice_fusion, f32[128]{0:T(128)S(1)} %get-tuple-element.20, bf16[10240,384]{1,0:T(8,128)(2,1)} %constant_dynamic-update-slice_fusion.2, bf16[128,384]{0,1:T(8,128)(2,1)S(1)} %copy-done.5, f32[10240,128]{1,0:T(8,128)} %copy-done.1, ...), kind=kOutput, calls=%fused_computation.89 | convolution fusion | flops 680296448 | bytes 10562560 | tf_op jit(solution)/shard_map/dot_general | solution.py:85
  429.0 6.6 %fusion.90 = bf16[128,128]{0,1:T(8,128)(2,1)S(1)} fusion(bf16[10240,384]{1,0:T(8,128)(2,1)} %constant_dynamic-update-slice_fusion, f32[128]{0:T(128)S(1)} %get-tuple-element.19, bf16[10240,384]{1,0:T(8,128)(2,1)} %constant_dynamic-update-slice_fusion.2, bf16[128,384]{0,1:T(8,128)(2,1)S(1)} %copy-done.5, f32[10240,128]{1,0:T(8,128)} %copy-done.2, ...), kind=kOutput, calls=%fused_computation.90 | convolution fusion | flops 680296448 | bytes 10562560 | tf_op jit(solution)/shard_map/dot_general | solution.py:85
  435.6 6.9 %fusion.93 = bf16[128,128]{0,1:T(8,128)(2,1)S(1)} fusion(bf16[10240,384]{1,0:T(8,128)(2,1)} %constant_dynamic-update-slice_fusion, f32[128]{0:T(128)S(1)} %get-tuple-element.18, bf16[10240,384]{1,0:T(8,128)(2,1)} %constant_dynamic-update-slice_fusion.2, bf16[128,384]{0,1:T(8,128)(2,1)S(1)} %copy-done.5, f32[10240,128]{1,0:T(8,128)} %copy-done.3, ...), kind=kOutput, calls=%fused_computation.91 | convolution fusion | flops 680296448 | bytes 10562560 | tf_op jit(solution)/shard_map/dot_general | solution.py:85
  442.5 49.4 %all-gather.17.cloned.1.call-done = bf16[8192,384]{0,1:T(8,128)(2,1)} async-done(((bf16[128,384]{0,1:T(8,128)(2,1)}), bf16[8192,384]{0,1:T(8,128)(2,1)}) %all-gather.17.cloned.1.call-update) | async-done | bytes 6291472 | tf_op jit(solution)/shard_map/all_gather | solution.py:112
  491.9 4.5 fusion.48
  496.4 4.6 fusion.54
  501.0 4.6 fusion.60
  509.1 3.4 fusion.84
  519.5 36.5 %all-reduce.4.cloned.1.call-done = bf16[128,3072]{1,0:T(8,128)(2,1)} async-done(((bf16[128,3072]{1,0:T(8,128)(2,1)}), bf16[128,3072]{1,0:T(8,128)(2,1)}) %all-reduce.4.cloned.1.call-update) | async-done | bytes 786448 | tf_op jit(solution)/shard_map/psum | solution.py:97
  (82 shorter events, 43.6 us)
Async XLA Ops:
  7.2 16.6 %copy-start = (bf16[384,3072]{1,0:T(8,128)(2,1)S(1)}, bf16[384,3072]{1,0:T(8,128)(2,1)}, u32[]{:S(2)}) copy-start(bf16[384,3072]{1,0:T(8,128)(2,1)} %param.16) | copy-start | bytes 7077892
  7.2 89.0 %all-gather.7.cloned.1.call-start = ((), (), s32[]{:S(2)}) async-start(), calls=%async_computation | async-start | bytes 6389760 | tf_op jit(solution)/shard_map/all_gather | solution.py:52
  7.9 164.6 %all-gather.9.cloned.1.call-start = ((), (), s32[]{:S(2)}) async-start(), calls=%async_computation.1 | async-start | bytes 1597440 | tf_op jit(solution)/shard_map/all_gather | solution.py:54
  8.7 245.4 %all-gather.11.cloned.1.call-start = ((), (), s32[]{:S(2)}) async-start(), calls=%async_computation.2 | async-start | bytes 6389760 | tf_op jit(solution)/shard_map/all_gather | solution.py:53
  9.4 320.9 %all-gather.13.cloned.1.call-start = ((), (), s32[]{:S(2)}) async-start(), calls=%async_computation.3 | async-start | bytes 1597440 | tf_op jit(solution)/shard_map/all_gather | solution.py:55
  10.0 401.7 %all-gather.15.cloned.1.call-start = ((), (), s32[]{:S(2)}) async-start(), calls=%async_computation.5 | async-start | bytes 6389760 | tf_op jit(solution)/shard_map/all_gather | solution.py:111
  10.6 481.3 %all-gather.17.cloned.1.call-start = ((), (), s32[]{:S(2)}) async-start(), calls=%async_computation.6 | async-start | bytes 6389760 | tf_op jit(solution)/shard_map/all_gather | solution.py:112
  25.2 530.8 %all-reduce.4.cloned.1.call-start = ((), (), s32[]{:S(2)}) async-start(), calls=%async_computation.4 | async-start | bytes 1572864 | tf_op jit(solution)/shard_map/psum | solution.py:97
  30.8 144.4 %copy-start.6 = (bf16[128,384]{1,0:T(8,128)(2,1)S(1)}, bf16[128,384]{1,0:T(8,128)(2,1)}, u32[]{:S(2)}) copy-start(bf16[128,384]{1,0:T(8,128)(2,1)} %param.9) | copy-start | bytes 294916
  175.2 9.3 %copy-start.4 = (bf16[10240,384]{1,0:T(8,128)(2,1)S(1)}, bf16[10240,384]{1,0:T(8,128)(2,1)}, u32[]{:S(2)}) copy-start(bf16[10240,384]{1,0:T(8,128)(2,1)} %constant_dynamic-update-slice_fusion) | copy-start | bytes 23592964
  183.1 3.0 copy-start.1
  186.1 3.0 copy-start.2
  189.1 2.3 copy-start.3
  330.3 11.1 %slice-start = ((s8[5242880]{0:T(1024)(128)(4,1)}), s8[1048576]{0:T(1024)(128)(4,1)S(1)}, s32[]{:S(2)}) async-start(s8[5242880]{0:T(1024)(128)(4,1)} %bitcast.42), calls=%async_computation.7 | async-start | bytes 2097152
  333.1 8.3 %slice-start.1 = ((s8[5242880]{0:T(1024)(128)(4,1)}), s8[4194304]{0:T(1024)(128)(4,1)S(1)}, s32[]{:S(2)}) async-start(s8[5242880]{0:T(1024)(128)(4,1)} %bitcast.42), calls=%async_computation.8 | async-start | bytes 8388608
  333.1 16.8 %slice-start.2 = ((s8[5242880]{0:T(1024)(128)(4,1)}), s8[4194304]{0:T(1024)(128)(4,1)S(1)}, s32[]{:S(2)}) async-start(s8[5242880]{0:T(1024)(128)(4,1)} %bitcast.44), calls=%async_computation.9 | async-start | bytes 8388608
  341.4 8.5 %slice-start.3 = ((s8[5242880]{0:T(1024)(128)(4,1)}), s8[1048576]{0:T(1024)(128)(4,1)S(1)}, s32[]{:S(2)}) async-start(s8[5242880]{0:T(1024)(128)(4,1)} %bitcast.44), calls=%async_computation.10 | async-start | bytes 2097152
  341.4 8.5 %copy-start.5 = (bf16[128,384]{0,1:T(8,128)(2,1)S(1)}, bf16[128,384]{0,1:T(8,128)(2,1)}, u32[]{:S(2)}) copy-start(bf16[128,384]{0,1:T(8,128)(2,1)} %convolution_convert_fusion.1) | copy-start | bytes 294916
  411.7 4.6 copy-start.7
  509.1 6.6 %copy-start.8 = (bf16[160,8192]{1,0:T(8,128)(2,1)S(1)}, bf16[160,8192]{1,0:T(8,128)(2,1)}, u32[]{:S(2)}) copy-start(bf16[160,8192]{1,0:T(8,128)(2,1)} %fusion.23) | copy-start | bytes 7864324
Sparse Core Ops, SparseCore 0:
  10.8 85.3 all-gather.6
  98.9 73.5 all-gather.8
  175.2 78.7 all-gather.10
  256.7 73.5 all-gather.12
  332.9 78.7 all-gather.14
  414.8 77.0 all-gather.16
  508.5 47.4 all-reduce.3
where the time goes:
time: 566 us; the launch traced here: 564 us
  waiting for transfers between devices  313 us (55%)
  blocking collectives  110 us (19%)
  matrix products  92.4 us (16%)
  local copies, waits for them, and re-layouts  26.1 us (5%)
  between operations  14.4 us (3%)
  other arithmetic  8.6 us (2%)
    all_gather x1, waiting for transfers between devices, shards(): lax.all_gather(hist_k, 'ctx', axis=0, tiled=True)  70.3 us
    all_gather x1, waiting for transfers between devices, shards(): lax.all_gather(hist_v, 'ctx', axis=0, tiled=True)  70.2 us
    all_gather x1, waiting for transfers between devices, shards(): lax.all_gather(sec_k, 'ctx', axis=0, tiled=True)  65.4 us
    all_gather x1, waiting for transfers between devices, shards(): dattn_piece = lax.all_gather(d_attn, 'ctx', axis=0, tiled=True)  49.4 us
    all_gather x1, blocking collectives, shards(): lax.all_gather(jnp.stack(log_totals, 0), 'ctx', axis=1, tiled=True)  48.5 us
    all_gather x1, blocking collectives, shards(): lax.all_gather(jnp.stack(row_deltas, 0), 'ctx', axis=1, tiled=True)  48.3 us
    psum x1, waiting for transfers between devices, shards(): lax.psum(partial_out.astype(jnp.bfloat16), 'head').astype(jnp.float32)  36.5 us
    dot_general x3, matrix products, shards(): jnp.dot(prob_h, value_h, preferred_element_type=jnp.float32)  25.1 us
  transfers between devices with their start and end apart: 7, of which 7 were waited for; matrix products, arithmetic and copies ran while one was open for 19% of the time, Pallas kernels for 0%

commit v1 on v0

v1 whole, which is shorter than its diff:
```python
import functools
import math

import jax
import jax.numpy as jnp
from jax import lax
from jax.experimental import pallas as pl
from jax.experimental.pallas import tpu as pltpu
from jax.sharding import PartitionSpec as P

HDIM = 128
FTOK = 16
FMAX = 2
NEG_FILL = -1e30
MESH = pl.DeviceIdType.MESH

NZ, NY, NC, NX = 8, 4, 2, 4
HEADS = 3
ROWS = 128
HCAP = 32
QT = NZ * ROWS
SECT = NY * NC * ROWS
HIST = NY * NC * HCAP
KT = SECT + HIST
CHUNK = 256
NCHUNK = KT // CHUNK
WIDTH = HEADS * HDIM
OCOLS = 768
BF = jnp.bfloat16
F32 = jnp.float32

OFFS = (0, 1, -1, 2, -2, 3, -3, 4)
SLOT = {off: i for i, off in enumerate(OFFS)}
SLOT[-4] = SLOT[4]

SCALE = 1.0 / math.sqrt(HDIM)
SCALE2 = SCALE * math.log2(math.e)


def dot_nn(a, b):
    return lax.dot_general(a, b, (((1,), (0,)), ((), ())), preferred_element_type=F32)


def dot_nt(a, b):
    return lax.dot_general(a, b, (((1,), (1,)), ((), ())), preferred_element_type=F32)


class Sems:
    def __init__(self):
        self.names = {}

    def __call__(self, *name):
        return self.names.setdefault(name, len(self.names))


N_SEMS = 160


def kernel(
    q_ref, k_ref, v_ref, hk_ref, hv_ref, lev_ref, cnt_ref, w_hbm, g_ref,
    out_ref, gq_ref, gk_ref, gv_ref, ghk_ref, ghv_ref,
    q_all, k_all, v_all, kt, vt, w_all, g_all, do_all, dop, bias,
    s_scr, p_scr, o_scr, ds_scr, dq_scr, dkv_scr,
    st, st_recv, ret, ret_recv, cd,
    o_send, o_recv, dq_send, dq_recv,
    r1_sec, r1_hist, t_sec, t_hist, r2_sec, r2_hist,
    po_send, po_recv,
    send_sem, recv_sem, w_sem,
):
    ctx = lax.axis_index("ctx")
    x = lax.axis_index("head")
    core = lax.rem(ctx, NC)
    y = lax.rem(ctx // NC, NY)
    z = ctx // (NC * NY)
    way = 1 - 2 * core

    def at_z(off):
        return (lax.rem(z + off * way + 2 * NZ, NZ) * NY + y) * NC + core

    def at_y(dy):
        return (z * NY + lax.rem(y + dy, NY)) * NC + core

    def at_x(dx):
        return lax.rem(x + dx, NX)

    sibling = (z * NY + y) * NC + (1 - core)

    sems = Sems()
    sent = []

    def send(src, dst, name, to_ctx=None, to_head=None):
        i = sems(*name)
        copy = pltpu.make_async_remote_copy(
            src_ref=src, dst_ref=dst, send_sem=send_sem.at[i], recv_sem=recv_sem.at[i],
            device_id=(ctx if to_ctx is None else to_ctx, x if to_head is None else to_head),
            device_id_type=MESH,
        )
        copy.start()
        sent.append(copy)

    def recv(dst, name):
        i = sems(*name)
        pltpu.make_async_remote_copy(
            src_ref=dst, dst_ref=dst, send_sem=send_sem.at[i], recv_sem=recv_sem.at[i],
            device_id=(sibling, x), device_id_type=MESH,
        ).wait_recv()

    barrier = pltpu.get_barrier_semaphore()
    peers = [(at_z(o), x) for o in OFFS[1:]]
    peers += [(at_y(d), x) for d in range(1, NY)]
    peers += [(sibling, x)]
    peers += [(ctx, at_x(d)) for d in range(1, NX)]
    for peer in peers:
        pl.semaphore_signal(barrier, inc=1, device_id=peer, device_id_type=MESH)

    w_copy = pltpu.make_async_copy(w_hbm, w_all, w_sem)
    w_copy.start()
    for h in range(HEADS):
        cols = slice(h * HDIM, (h + 1) * HDIM)
        q_all[h, 0:ROWS, :] = q_ref[:, cols]
        k_all[h, 0:ROWS, :] = k_ref[:, cols]
        k_all[h, SECT : SECT + HCAP, :] = hk_ref[:, cols]
        v_all[h, 0:ROWS, :] = v_ref[:, cols]
        v_all[h, SECT : SECT + HCAP, :] = hv_ref[:, cols]

    pl.semaphore_wait(barrier, len(peers))

    def ring_send(buf, tag, off, up):
        there = off - 1 if up else off + 1
        src = buf.at[:, pl.ds(SLOT[off] * ROWS, ROWS), :]
        dst = buf.at[:, pl.ds(SLOT[there] * ROWS, ROWS), :]
        send(src, dst, (tag, there), to_ctx=at_z(1 if up else -1))

    def ring_recv(buf, tag, off):
        recv(buf.at[:, pl.ds(SLOT[off] * ROWS, ROWS), :], (tag, off))

    def gather_step(buf, tag, step):
        if step > 1:
            ring_recv(buf, tag, step - 1)
        ring_send(buf, tag, step - 1, False)
        if step < 4:
            if step > 1:
                ring_recv(buf, tag, 1 - step)
            ring_send(buf, tag, 1 - step, True)

    gather_step(q_all, "q", 1)
    for dx in range(1, NX):
        there = (NX - dx) % NX
        send(g_ref, g_all.at[there], ("g", there), to_head=at_x(dx))
    pieces = ((0, ROWS), (SECT, HCAP))
    for tag, buf in (("k", k_all), ("v", v_all)):
        for dy in (1, 3, 2):
            there = (NY - dy) % NY
            for start, size in pieces:
                src = buf.at[:, pl.ds(start, size), :]
                dst = buf.at[:, pl.ds(start + there * size, size), :]
                send(src, dst, (tag, there, start), to_ctx=at_y(dy))

    def to_sibling(tag, buf):
        for dy in (1, 3, 2):
            for start, size in pieces:
                recv(buf.at[:, pl.ds(start + dy * size, size), :], (tag, dy, start))
        for start, size in pieces:
            src = buf.at[:, pl.ds(start, NY * size), :]
            dst = buf.at[:, pl.ds(start + NY * size, NY * size), :]
            send(src, dst, (tag, "sib", start), to_ctx=sibling)

    def from_sibling(tag, buf):
        for start, size in pieces:
            recv(buf.at[:, pl.ds(start + NY * size, NY * size), :], (tag, "sib", start))

    row = lax.broadcasted_iota(jnp.int32, (HIST, CHUNK), 0)
    limit = jnp.zeros((HIST, CHUNK), jnp.int32)
    for dc in range(NC):
        for dy in range(NY):
            owner = (z * NY + lax.rem(y + dy, NY)) * NC + (core if dc == 0 else 1 - core)
            tokens = jnp.int32(0)
            for f in range(FMAX):
                level = lev_ref[owner, f]
                size = lax.shift_right_logical(jnp.int32(FTOK), 2 * level)
                tokens = tokens + jnp.where(f < cnt_ref[owner], size, 0)
            j = dc * NY + dy
            mine = (row >= j * HCAP) & (row < (j + 1) * HCAP)
            limit = jnp.where(mine, tokens + j * HCAP, limit)
    bias[...] = jnp.where(row < limit, 0.0, NEG_FILL)

    gather_step(q_all, "q", 2)
    to_sibling("k", k_all)
    gather_step(q_all, "q", 3)

    w_copy.wait()

    def w_cols(dx):
        return w_all[:, pl.ds(pl.multiple_of(at_x(dx) * OCOLS, OCOLS), OCOLS)]

    d_attn = dot_nt(g_ref[...], w_cols(0))
    to_sibling("v", v_all)
    for dx in (1, 3, 2):
        recv(g_all.at[dx], ("g", dx))
        d_attn += dot_nt(g_all[dx], w_cols(dx))
    for h in range(HEADS):
        do_all[h, 0:ROWS, :] = d_attn[:, h * HDIM : (h + 1) * HDIM].astype(BF)
    gather_step(do_all, "d", 1)
    gather_step(q_all, "q", 4)

    from_sibling("k", k_all)
    from_sibling("v", v_all)

    def turn(h, _):
        for i in range(KT // HDIM):
            rows = slice(i * HDIM, (i + 1) * HDIM)
            vt[h, :, rows] = v_all[h, rows, :].T
            kt[h, :, rows] = k_all[h, rows, :].T
        return 0

    lax.fori_loop(0, HEADS, turn, 0)

    def forward(pair):
        cols = slice(pair * CHUNK, (pair + 1) * CHUNK)

        def one(h, _):
            query = q_all[h, cols, :]
            top = None
            for c in range(NCHUNK):
                rows = slice(c * CHUNK, (c + 1) * CHUNK)
                s = dot_nt(k_all[h, rows, :], query)
                if c == NCHUNK - 1:
                    s = s + bias[...]
                s_scr[rows, :] = s
                part = jnp.max(s.reshape(CHUNK // 8, 8, CHUNK), axis=0)
                top = part if top is None else jnp.maximum(top, part)
            top = jnp.max(top, axis=0, keepdims=True) * SCALE2
            total = jnp.zeros((8, CHUNK), F32)
            for c in range(NCHUNK):
                rows = slice(c * CHUNK, (c + 1) * CHUNK)
                p = jnp.exp2(s_scr[rows, :] * SCALE2 - top)
                total += jnp.sum(p.reshape(CHUNK // 8, 8, CHUNK), axis=0)
                p_scr[h, rows, cols] = p.astype(BF)
            total = jnp.sum(total, axis=0, keepdims=True)
            o_scr[h, :, cols] = dot_nn(vt[h], p_scr[h, :, cols])
            for i in range(2):
                half = slice(i * ROWS, (i + 1) * ROWS)
                st[2 * pair + i, pl.ds(h, 1), :] = top[:, half]
                st[2 * pair + i, pl.ds(HEADS + h, 1), :] = total[:, half]
            return 0

        lax.fori_loop(0, HEADS, one, 0)

    forward(0)
    forward(1)
    gather_step(do_all, "d", 2)
    forward(2)
    gather_step(do_all, "d", 3)
    ring_recv(q_all, "q", -3)
    ring_recv(q_all, "q", 4)
    forward(3)
    gather_step(do_all, "d", 4)

    eye = lax.broadcasted_iota(jnp.int32, (ROWS, ROWS), 0) == lax.broadcasted_iota(
        jnp.int32, (ROWS, ROWS), 1
    )

    def share(slot):
        rows = slice(slot * ROWS, (slot + 1) * ROWS)
        for h in range(HEADS):
            both = dot_nn(do_all[h, rows, :], o_scr[h, :, rows].astype(BF))
            st[slot, 2 * HEADS + h : 2 * HEADS + h + 1, :] = jnp.sum(
                jnp.where(eye, both, 0.0), axis=0, keepdims=True
            )

    for off in OFFS:
        if off in (-3, 4):
            ring_recv(do_all, "d", off)
        share(SLOT[off])
        if off != 0:
            there = SLOT[-off]
            send(st.at[SLOT[off]], st_recv.at[there], ("st", there), to_ctx=at_z(off))
    for slot in range(1, NZ):
        recv(st_recv.at[slot], ("st", slot))
    parts = [st[0]] + [st_recv[slot] for slot in range(1, NZ)]
    peak = functools.reduce(jnp.maximum, [p[0:HEADS] for p in parts])
    weights = [jnp.exp2(p[0:HEADS] - peak) for p in parts]
    whole = sum(w * p[HEADS : 2 * HEADS] for w, p in zip(weights, parts))
    delta = sum(w * p[2 * HEADS : 3 * HEADS] for w, p in zip(weights, parts)) / whole
    ret[0:HEADS, :] = peak + jnp.log2(whole)
    ret[HEADS : 2 * HEADS, :] = delta
    for off in OFFS[1:]:
        there = SLOT[-off]
        send(ret, ret_recv.at[there], ("ret", there), to_ctx=at_z(off))

    def settle(slot):
        back = ret[...] if slot == 0 else ret_recv[slot]
        factor = jnp.exp2(st[slot, 0:HEADS, :] - back[0:HEADS])
        cd[slot, 0:HEADS, :] = factor
        cd[slot, HEADS : 2 * HEADS, :] = factor * back[HEADS : 2 * HEADS]
        rows = slice(slot * ROWS, (slot + 1) * ROWS)
        for h in range(HEADS):
            column = jnp.broadcast_to(factor[h : h + 1], (ROWS, ROWS)).T
            dop[h, rows, :] = (do_all[h, rows, :].astype(F32) * column).astype(BF)

    for slot in range(NZ):
        if slot:
            recv(ret_recv.at[slot], ("ret", slot))
        settle(slot)

    class RingSum:
        def __init__(self, tag, term, out_buf, in_buf):
            self.tag, self.term, self.out_buf, self.in_buf = tag, term, out_buf, in_buf

        def pass_on(self, off, up, first):
            i = off - 1 if up else 3 - off
            value = self.term(off)
            if not first:
                j = SLOT[off] if up else SLOT[off]
                recv(self.in_buf.at[j], (self.tag, up, off))
                value = value + self.in_buf[j].astype(F32)
            slot = SLOT[off]
            self.out_buf[slot] = value.astype(BF)
            there = off - 1 if up else off + 1
            to = SLOT[4] if there == 0 and not up else SLOT[there]
            send(
                self.out_buf.at[slot], self.in_buf.at[to], (self.tag, up, there),
                to_ctx=at_z(1 if up else -1),
            )

        def step(self, n):
            self.pass_on(5 - n, True, n == 1)
            if n < 4:
                self.pass_on(n - 4, False, n == 1)

        def finish(self):
            recv(self.in_buf.at[SLOT[0]], (self.tag, True, 0))
            recv(self.in_buf.at[SLOT[4]], (self.tag, False, 0))
            both = self.in_buf[SLOT[0]].astype(F32) + self.in_buf[SLOT[4]].astype(F32)
            return self.term(0) + both

    def o_term(off):
        slot = SLOT[off]
        rows = slice(slot * ROWS, (slot + 1) * ROWS)
        return jnp.stack([o_scr[h, :, rows] * cd[slot, h : h + 1, :] for h in range(HEADS)])

    def dq_term(h):
        def term(off):
            slot = SLOT[off]
            return dq_scr[h, :, slot * ROWS : (slot + 1) * ROWS]

        return term

    o_sum = RingSum("o", o_term, o_send, o_recv)
    dq_sums = [RingSum("dq%d" % h, dq_term(h), dq_send.at[h], dq_recv.at[h]) for h in range(HEADS)]

    def backward_keys(h, first, last):
        def one(c, _):
            rows = pl.ds(pl.multiple_of(c * CHUNK, CHUNK), CHUNK)
            value = v_all[h, rows, :]
            for pair in range(4):
                cols = slice(pair * CHUNK, (pair + 1) * CHUNK)
                dp = dot_nt(value, dop[h, cols, :])
                a, b = 2 * pair, 2 * pair + 1
                d = HEADS + h
                minus = jnp.concatenate([cd[a, d : d + 1, :], cd[b, d : d + 1, :]], axis=1)
                ds = p_scr[h, rows, cols].astype(F32) * (dp - minus)
                ds_scr[rows, cols] = ds.astype(BF)
            dkv_scr[h, rows, 0:HDIM] = dot_nn(ds_scr[rows, :], q_all[h]).astype(BF)
            dkv_scr[h, rows, HDIM : 2 * HDIM] = dot_nn(p_scr[h, rows, :], dop[h]).astype(BF)
            return 0

        lax.fori_loop(first, last, one, 0)

    def backward_queries(h):
        for pair in range(4):
            cols = slice(pair * CHUNK, (pair + 1) * CHUNK)
            dq_scr[h, :, cols] = dot_nn(kt[h], ds_scr[:, cols])

    def keys_to_sibling(h):
        send(dkv_scr.at[h, pl.ds(SECT // 2, SECT // 2)], r1_sec.at[h], ("r1s", h), to_ctx=sibling)
        src = dkv_scr.at[h, pl.ds(SECT + HIST // 2, HIST // 2)]
        send(src, r1_hist.at[h], ("r1h", h), to_ctx=sibling)

    def keys_along_y(h):
        recv(r1_sec.at[h], ("r1s", h))
        recv(r1_hist.at[h], ("r1h", h))
        for dy in (1, 3, 2, 0):
            there = (NY - dy) % NY
            for name, mine, got, total, into, start, size in (
                ("r2s", dkv_scr, r1_sec, t_sec, r2_sec, 0, ROWS),
                ("r2h", dkv_scr, r1_hist, t_hist, r2_hist, SECT, HCAP),
            ):
                rows = slice(dy * size, (dy + 1) * size)
                own = mine[h, start + dy * size : start + (dy + 1) * size, :].astype(F32)
                total[h, rows, :] = (own + got[h, rows, :].astype(F32)).astype(BF)
                if dy:
                    src = total.at[h, pl.ds(dy * size, size)]
                    send(src, into.at[h, there], (name, h, there), to_ctx=at_y(dy))

    def keys_finish(h):
        cols = slice(h * HDIM, (h + 1) * HDIM)
        for name, total, into, size, k_out, v_out in (
            ("r2s", t_sec, r2_sec, ROWS, gk_ref, gv_ref),
            ("r2h", t_hist, r2_hist, HCAP, ghk_ref, ghv_ref),
        ):
            value = total[h, 0:size, :].astype(F32)
            for dy in range(1, NY):
                recv(into.at[h, dy], (name, h, dy))
                value = value + into[h, dy].astype(F32)
            k_out[:, cols] = (value[:, 0:HDIM] * SCALE).astype(BF)
            v_out[:, cols] = value[:, HDIM : 2 * HDIM].astype(BF)

    def queries_finish(h):
        total = dq_sums[h].finish() * SCALE
        gq_ref[:, h * HDIM : (h + 1) * HDIM] = total.T.astype(BF)

    o_sum.step(1)
    backward_keys(0, 0, 3)
    o_sum.step(2)
    backward_keys(0, 3, 5)
    backward_queries(0)
    keys_to_sibling(0)
    dq_sums[0].step(1)
    o_sum.step(3)
    backward_keys(1, 0, 3)
    dq_sums[0].step(2)
    o_sum.step(4)
    keys_along_y(0)
    backward_keys(1, 3, 5)
    backward_queries(1)
    keys_to_sibling(1)
    dq_sums[1].step(1)
    dq_sums[0].step(3)
    total_o = o_sum.finish()
    attn = jnp.concatenate([total_o[h].T for h in range(HEADS)], axis=1).astype(BF)
    for dx in (2, 1, 3):
        there = (NX - dx) % NX
        po_send[dx] = dot_nn(attn, w_cols(dx)).astype(BF)
        send(po_send.at[dx], po_recv.at[there], ("po", there), to_head=at_x(dx))
    own_out = dot_nn(attn, w_cols(0))
    backward_keys(2, 0, 3)
    dq_sums[0].step(4)
    dq_sums[1].step(2)
    keys_along_y(1)
    keys_finish(0)
    backward_keys(2, 3, 5)
    backward_queries(2)
    keys_to_sibling(2)
    dq_sums[2].step(1)
    dq_sums[1].step(3)
    queries_finish(0)
    keys_along_y(2)
    dq_sums[2].step(2)
    dq_sums[1].step(4)
    keys_finish(1)
    dq_sums[2].step(3)
    queries_finish(1)
    dq_sums[2].step(4)
    for dx in (1, 3, 2):
        recv(po_recv.at[dx], ("po", dx))
        own_out += po_recv[dx].astype(F32)
    out_ref[...] = own_out.astype(BF)
    keys_finish(2)
    queries_finish(2)

    for copy in sent:
        copy.wait_send()
    assert len(sems.names) <= N_SEMS, len(sems.names)


def shards(sec_q, sec_k, sec_v, hist_k, hist_v, frame_levels, frame_counts, w_out, grad_out):
    vmem = pl.BlockSpec(memory_space=pltpu.VMEM)
    smem = pl.BlockSpec(memory_space=pltpu.SMEM)
    anywhere = pl.BlockSpec(memory_space=pl.ANY)
    scratch = [
        pltpu.VMEM((HEADS, QT, HDIM), BF),
        pltpu.VMEM((HEADS, KT, HDIM), BF),
        pltpu.VMEM((HEADS, KT, HDIM), BF),
        pltpu.VMEM((HEADS, HDIM, KT), BF),
        pltpu.VMEM((HEADS, HDIM, KT), BF),
        pltpu.VMEM((WIDTH, NX * OCOLS), BF),
        pltpu.VMEM((NX, ROWS, OCOLS), BF),
        pltpu.VMEM((HEADS, QT, HDIM), BF),
        pltpu.VMEM((HEADS, QT, HDIM), BF),
        pltpu.VMEM((HIST, CHUNK), F32),
        pltpu.VMEM((KT, CHUNK), F32),
        pltpu.VMEM((HEADS, KT, QT), BF),
        pltpu.VMEM((HEADS, HDIM, QT), F32),
        pltpu.VMEM((KT, QT), BF),
        pltpu.VMEM((HEADS, HDIM, QT), F32),
        pltpu.VMEM((HEADS, KT, 2 * HDIM), BF),
        pltpu.VMEM((NZ, 16, ROWS), F32),
        pltpu.VMEM((NZ, 16, ROWS), F32),
        pltpu.VMEM((8, ROWS), F32),
        pltpu.VMEM((NZ, 8, ROWS), F32),
        pltpu.VMEM((NZ, 8, ROWS), F32),
        pltpu.VMEM((NZ, HEADS, HDIM, ROWS), BF),
        pltpu.VMEM((NZ, HEADS, HDIM, ROWS), BF),
        pltpu.VMEM((HEADS, NZ, HDIM, ROWS), BF),
        pltpu.VMEM((HEADS, NZ, HDIM, ROWS), BF),
        pltpu.VMEM((HEADS, SECT // 2, 2 * HDIM), BF),
        pltpu.VMEM((HEADS, HIST // 2, 2 * HDIM), BF),
        pltpu.VMEM((HEADS, SECT // 2, 2 * HDIM), BF),
        pltpu.VMEM((HEADS, HIST // 2, 2 * HDIM), BF),
        pltpu.VMEM((HEADS, NY, ROWS, 2 * HDIM), BF),
        pltpu.VMEM((HEADS, NY, HCAP, 2 * HDIM), BF),
        pltpu.VMEM((NX, ROWS, OCOLS), BF),
        pltpu.VMEM((NX, ROWS, OCOLS), BF),
        pltpu.SemaphoreType.DMA((N_SEMS,)),
        pltpu.SemaphoreType.DMA((N_SEMS,)),
        pltpu.SemaphoreType.DMA(()),
    ]
    shapes = [
        jax.ShapeDtypeStruct((ROWS, OCOLS), BF),
        jax.ShapeDtypeStruct((ROWS, WIDTH), BF),
        jax.ShapeDtypeStruct((ROWS, WIDTH), BF),
        jax.ShapeDtypeStruct((ROWS, WIDTH), BF),
        jax.ShapeDtypeStruct((HCAP, WIDTH), BF),
        jax.ShapeDtypeStruct((HCAP, WIDTH), BF),
    ]
    return pl.pallas_call(
        kernel,
        out_shape=shapes,
        in_specs=[vmem] * 5 + [smem] * 2 + [anywhere, vmem],
        out_specs=[vmem] * 6,
        scratch_shapes=scratch,
        compiler_params=pltpu.CompilerParams(
            collective_id=0, has_side_effects=True, vmem_limit_bytes=60 * 1024 * 1024
        ),
    )(sec_q, sec_k, sec_v, hist_k, hist_v, frame_levels, frame_counts, w_out, grad_out)


def solution(mesh):
    both = P("ctx", "head")
    placed = (both, both, both, both, both, P(), P(), P("head", None), both)
    return jax.shard_map(
        shards, mesh=mesh, in_specs=placed, out_specs=(both,) * 6, check_vma=False
    )
```

time: 566 us -> 102 us (0.18)
  the two profiles are of different devices: /device:TPU:1 before, /device:TPU:38 now
where the time goes in v1:
time: 102 us
  Pallas kernels  90.8 us (89%)
  local copies, waits for them, and re-layouts  10.3 us (10%)
    pallas_call x1, Pallas kernels, shards(): pl.pallas_call(kernel, out_shape=shapes, in_specs=[vmem] * 5 + [smem] * 2...  90.8 us
    unnamed x7, local copies, waits for them, and re-layouts  10.3 us

profile of v1, /device:TPU:38, one launch (start us, length us, event | category | flops | bytes accessed | tf_op | source)
XLA Modules:
  0.0 101.7 jit_solution(442669243843347245)
XLA Ops:
  0.6 1.4 %copy.15.lev_ref = s32[64,2]{1,0:T(8,128)} copy(s32[64,2]{0,1:T(2,128)} %param.14) | data formatting | bytes 1024 | tf_op args[5]
  2.0 90.8 %shard_map.136 = (bf16[128,768]{1,0:T(8,128)(2,1)}, bf16[128,384]{1,0:T(8,128)(2,1)}, bf16[128,384]{1,0:T(8,128)(2,1)}, bf16[128,384]{1,0:T(8,128)(2,1)}, bf16[3...) custom-call(bf16[128,384]{1,0:T(8,128)(2,1)} %q_ref.1, bf16[128,384]{1,0:T(8,128)(2,1)} %k_ref.1, bf16[128,384]{1,0:T(8,128)(2,1)} %v_ref.1, ...), custom_call_target="tpu_custom_call" | custom-call | tf_op jit(solution)/shard_map/pallas_call | solution.py:517
  92.8 1.6 %copy.22 = bf16[128,768]{1,0:T(8,128)(2,1)} copy(bf16[128,768]{1,0:T(8,128)(2,1)} %get-tuple-element.12) | data formatting | bytes 393216
  94.4 1.5 %copy.23 = bf16[128,384]{1,0:T(8,128)(2,1)} copy(bf16[128,384]{1,0:T(8,128)(2,1)} %get-tuple-element.13) | data formatting | bytes 196608
  96.0 1.5 %copy.24 = bf16[128,384]{1,0:T(8,128)(2,1)} copy(bf16[128,384]{1,0:T(8,128)(2,1)} %get-tuple-element.14) | data formatting | bytes 196608
  97.5 1.5 %copy.25 = bf16[128,384]{1,0:T(8,128)(2,1)} copy(bf16[128,384]{1,0:T(8,128)(2,1)} %get-tuple-element.15) | data formatting | bytes 196608
  99.1 1.3 %copy.26 = bf16[32,384]{1,0:T(8,128)(2,1)} copy(bf16[32,384]{1,0:T(8,128)(2,1)} %get-tuple-element.16) | data formatting | bytes 49152
  100.4 1.3 %copy.27 = bf16[32,384]{1,0:T(8,128)(2,1)} copy(bf16[32,384]{1,0:T(8,128)(2,1)} %get-tuple-element.17) | data formatting | bytes 49152

commit v2 on v1

v2 whole, which is shorter than its diff:
```python
import functools
import math

import jax
import jax.numpy as jnp
from jax import lax
from jax.experimental import pallas as pl
from jax.experimental.pallas import tpu as pltpu
from jax.sharding import PartitionSpec as P

HDIM = 128
FTOK = 16
FMAX = 2
NEG_FILL = -1e30
MESH = pl.DeviceIdType.MESH

NZ, NY, NC, NX = 8, 4, 2, 4
HEADS = 3
ROWS = 128
HCAP = 32
QT = NZ * ROWS
SECT = NY * NC * ROWS
HIST = NY * NC * HCAP
KT = SECT + HIST
CHUNK = 256
NCHUNK = KT // CHUNK
WIDTH = HEADS * HDIM
OCOLS = 768
BF = jnp.bfloat16
F32 = jnp.float32

OFFS = (0, 1, -1, 2, -2, 3, -3, 4)
SLOT = {off: i for i, off in enumerate(OFFS)}
SLOT[-4] = SLOT[4]

SCALE = 1.0 / math.sqrt(HDIM)
SCALE2 = SCALE * math.log2(math.e)


def dot_nn(a, b):
    return lax.dot_general(a, b, (((1,), (0,)), ((), ())), preferred_element_type=F32)


def dot_nt(a, b):
    return lax.dot_general(a, b, (((1,), (1,)), ((), ())), preferred_element_type=F32)


class Sems:
    def __init__(self):
        self.names = {}

    def __call__(self, *name):
        return self.names.setdefault(name, len(self.names))


N_SEMS = 224


def kernel(
    q_ref, k_ref, v_ref, hk_ref, hv_ref, lev_ref, cnt_ref, w_hbm, g_ref,
    out_ref, gq_ref, gk_ref, gv_ref, ghk_ref, ghv_ref,
    q_all, kv_all, kt, vt, w_all, g_all, do_all, dop, bias,
    s_scr, p_scr, o_part, ds_scr, dq_part, dkv_scr,
    st, ret, ret_recv, cd,
    o_mid, o_in, st_mid, st_in, dq_mid, dq_in,
    r1_sec, r1_hist, t_sec, t_hist, r2_sec, r2_hist,
    po_send, po_recv,
    send_sem, recv_sem, w_sem,
):
    ctx = lax.axis_index("ctx")
    x = lax.axis_index("head")
    core = lax.rem(ctx, NC)
    y = lax.rem(ctx // NC, NY)
    z = ctx // (NC * NY)
    way = 1 - 2 * core

    def at_z(off):
        return (lax.rem(z + off * way + 2 * NZ, NZ) * NY + y) * NC + core

    def at_y(dy):
        return (z * NY + lax.rem(y + dy, NY)) * NC + core

    def at_x(dx):
        return lax.rem(x + dx, NX)

    sibling = (z * NY + y) * NC + (1 - core)

    sems = Sems()
    sent = []

    def send(src, dst, name, to_ctx=None, to_head=None):
        i = sems(*name)
        copy = pltpu.make_async_remote_copy(
            src_ref=src, dst_ref=dst, send_sem=send_sem.at[i], recv_sem=recv_sem.at[i],
            device_id=(ctx if to_ctx is None else to_ctx, x if to_head is None else to_head),
            device_id_type=MESH,
        )
        copy.start()
        sent.append(copy)

    def recv(dst, name):
        i = sems(*name)
        pltpu.make_async_remote_copy(
            src_ref=dst, dst_ref=dst, send_sem=send_sem.at[i], recv_sem=recv_sem.at[i],
            device_id=(sibling, x), device_id_type=MESH,
        ).wait_recv()

    barrier = pltpu.get_barrier_semaphore()
    peers = [(at_z(o), x) for o in OFFS[1:]]
    peers += [(at_y(d), x) for d in range(1, NY)]
    peers += [(sibling, x)]
    peers += [(ctx, at_x(d)) for d in range(1, NX)]
    for peer in peers:
        pl.semaphore_signal(barrier, inc=1, device_id=peer, device_id_type=MESH)

    w_copy = pltpu.make_async_copy(w_hbm, w_all, w_sem)
    w_copy.start()
    for h in range(HEADS):
        cols = slice(h * HDIM, (h + 1) * HDIM)
        q_all[h, 0:ROWS, :] = q_ref[:, cols]
        kv_all[h, 0, 0:ROWS, :] = k_ref[:, cols]
        kv_all[h, 0, SECT : SECT + HCAP, :] = hk_ref[:, cols]
        kv_all[h, 1, 0:ROWS, :] = v_ref[:, cols]
        kv_all[h, 1, SECT : SECT + HCAP, :] = hv_ref[:, cols]

    pl.semaphore_wait(barrier, len(peers))

    def z_slot(buf, h, off):
        return buf.at[h, pl.ds(SLOT[off] * ROWS, ROWS), :]

    def z_send(buf, tag, h, off, there, to):
        send(z_slot(buf, h, off), z_slot(buf, h, there), (tag, h, there), to_ctx=at_z(to))

    def z_recv(buf, tag, h, *offs):
        for off in offs:
            recv(z_slot(buf, h, off), (tag, h, off))

    def z_first(buf, tag, h):
        for off in (2, -2, 1, -1):
            z_send(buf, tag, h, 0, -off, off)

    def z_second(buf, tag, h):
        z_recv(buf, tag, h, 2)
        z_send(buf, tag, h, 2, 4, -2)
        z_send(buf, tag, h, 2, 3, -1)
        z_recv(buf, tag, h, -2)
        z_send(buf, tag, h, -2, -3, 1)

    def z_rest(buf, tag, h):
        z_recv(buf, tag, h, 1, -1, 3, -3, 4)

    pieces = ((0, ROWS), (SECT, HCAP))

    def kv_first(h):
        for dy in (2, 1, 3):
            there = (NY - dy) % NY
            for start, size in pieces:
                src = kv_all.at[h, :, pl.ds(start, size), :]
                dst = kv_all.at[h, :, pl.ds(start + there * size, size), :]
                send(src, dst, ("kv", h, there, start), to_ctx=at_y(dy))

    def kv_second(h):
        for dy in (1, 3, 2):
            for start, size in pieces:
                recv(kv_all.at[h, :, pl.ds(start + dy * size, size), :], ("kv", h, dy, start))
        for start, size in pieces:
            src = kv_all.at[h, :, pl.ds(start, NY * size), :]
            dst = kv_all.at[h, :, pl.ds(start + NY * size, NY * size), :]
            send(src, dst, ("kv", h, "sib", start), to_ctx=sibling)

    def kv_rest(h):
        for start, size in pieces:
            dst = kv_all.at[h, :, pl.ds(start + NY * size, NY * size), :]
            recv(dst, ("kv", h, "sib", start))
        for i in range(KT // HDIM):
            rows = slice(i * HDIM, (i + 1) * HDIM)
            kt[h, :, rows] = kv_all[h, 0, rows, :].T
            vt[h, :, rows] = kv_all[h, 1, rows, :].T

    for dx in (2, 1, 3):
        there = (NX - dx) % NX
        send(g_ref, g_all.at[there], ("g", there), to_head=at_x(dx))
    for h in range(HEADS):
        kv_first(h)
        z_first(q_all, "q", h)

    row = lax.broadcasted_iota(jnp.int32, (HIST, CHUNK), 0)
    limit = jnp.zeros((HIST, CHUNK), jnp.int32)
    for dc in range(NC):
        for dy in range(NY):
            owner = (z * NY + lax.rem(y + dy, NY)) * NC + (core if dc == 0 else 1 - core)
            tokens = jnp.int32(0)
            for f in range(FMAX):
                level = lev_ref[f, owner]
                size = lax.shift_right_logical(jnp.int32(FTOK), 2 * level)
                tokens = tokens + jnp.where(f < cnt_ref[owner], size, 0)
            j = dc * NY + dy
            mine = (row >= j * HCAP) & (row < (j + 1) * HCAP)
            limit = jnp.where(mine, tokens + j * HCAP, limit)
    bias[...] = jnp.where(row < limit, 0.0, NEG_FILL)

    def w_cols(dx):
        return w_all[:, pl.ds(pl.multiple_of(at_x(dx) * OCOLS, OCOLS), OCOLS)]

    def cotangent():
        w_copy.wait()
        d_attn = dot_nt(g_ref[...], w_cols(0))
        for dx in (1, 3, 2):
            recv(g_all.at[dx], ("g", dx))
            d_attn += dot_nt(g_all[dx], w_cols(dx))
        for h in range(HEADS):
            do_all[h, 0:ROWS, :] = d_attn[:, h * HDIM : (h + 1) * HDIM].astype(BF)
            z_first(do_all, "d", h)

    def forward(h, pair):
        cols = slice(pair * CHUNK, (pair + 1) * CHUNK)
        query = q_all[h, cols, :]
        top = None
        for c in range(NCHUNK):
            rows = slice(c * CHUNK, (c + 1) * CHUNK)
            s = dot_nt(kv_all[h, 0, rows, :], query)
            if c == NCHUNK - 1:
                s = s + bias[...]
            s_scr[rows, :] = s
            part = jnp.max(s.reshape(CHUNK // 8, 8, CHUNK), axis=0)
            top = part if top is None else jnp.maximum(top, part)
        top = jnp.max(top, axis=0, keepdims=True) * SCALE2
        total = jnp.zeros((8, CHUNK), F32)
        for c in range(NCHUNK):
            rows = slice(c * CHUNK, (c + 1) * CHUNK)
            p = jnp.exp2(s_scr[rows, :] * SCALE2 - top)
            total += jnp.sum(p.reshape(CHUNK // 8, 8, CHUNK), axis=0)
            p_scr[h, rows, cols] = p.astype(BF)
        total = jnp.sum(total, axis=0, keepdims=True)
        o = dot_nn(vt[h], p_scr[h, :, cols])
        for i in range(2):
            half = slice(i * ROWS, (i + 1) * ROWS)
            slot = 2 * pair + i
            o_part[h, slot] = o[:, half].astype(BF)
            st[h, slot, 0:1, :] = top[:, half]
            st[h, slot, 1:2, :] = total[:, half]

    INBOX = {("mid", 3): 0, ("mid", -3): 1, ("mid", 4): 2, 1: 3, -1: 4, 2: 5, -2: 6}

    def s_send(tag, h, srcs, boxes, key, to):
        i = INBOX[key]
        for n, (src, box) in enumerate(zip(srcs, boxes)):
            send(src, box.at[h, i], (tag, n, h, i), to_ctx=at_z(to))

    def s_recv(tag, h, boxes, key):
        i = INBOX[key]
        for n, box in enumerate(boxes):
            recv(box.at[h, i], (tag, n, h, i))
        return i

    def s_first(tag, h, parts, boxes):
        def at(off):
            return [p.at[h, SLOT[off]] for p in parts]

        s_send(tag, h, at(4), boxes, ("mid", 4), 2)
        s_send(tag, h, at(3), boxes, ("mid", 3), 1)
        s_send(tag, h, at(-3), boxes, ("mid", -3), -1)

    def s_near(tag, h, parts, boxes):
        for off in (1, -1):
            s_send(tag, h, [p.at[h, SLOT[off]] for p in parts], boxes, -off, off)

    o_parts, o_boxes = (o_part, st), (o_in, st_in)

    def merge(terms):
        peak = functools.reduce(jnp.maximum, [t[0] for t in terms])
        scales = [jnp.exp2(t[0] - peak) for t in terms]
        whole = sum(w * t[1] for w, t in zip(scales, terms))
        product = sum(w * t[2] for w, t in zip(scales, terms))
        return peak, whole, product

    def o_triple(h, slot):
        return st[h, slot, 0:1, :], st[h, slot, 1:2, :], o_part[h, slot].astype(F32)

    def o_arrived(h, key):
        i = s_recv("o", h, o_boxes, key)
        return st_in[h, i, 0:1, :], st_in[h, i, 1:2, :], o_in[h, i].astype(F32)

    def o_second(h):
        for n, off in enumerate((2, -2)):
            terms = [o_triple(h, SLOT[off]), o_arrived(h, ("mid", 3 if off > 0 else -3))]
            if off > 0:
                terms.append(o_arrived(h, ("mid", 4)))
            peak, whole, product = merge(terms)
            st_mid[h, n, 0:1, :] = peak
            st_mid[h, n, 1:2, :] = whole
            o_mid[h, n] = product.astype(BF)
            s_send("o", h, (o_mid.at[h, n], st_mid.at[h, n]), o_boxes, -off, off)

    attn = []

    def o_finish(h):
        terms = [o_triple(h, 0)] + [o_arrived(h, key) for key in (1, -1, 2, -2)]
        peak, whole, product = merge(terms)
        mine = (product / whole).T.astype(BF)
        attn.append(mine)
        both = mine.astype(F32) * do_all[h, 0:ROWS, :].astype(F32)
        delta = jnp.sum(both.T, axis=0, keepdims=True)
        ret[h, 0:1, :] = peak + jnp.log2(whole)
        ret[h, 1:2, :] = delta
        for off in OFFS[1:]:
            there = SLOT[-off]
            send(ret.at[h], ret_recv.at[h, there], ("ret", h, there), to_ctx=at_z(off))

    def settle(h):
        for slot in (0, 1, 2, 3, 4, 5, 6, 7):
            if slot:
                recv(ret_recv.at[h, slot], ("ret", h, slot))
            back = ret[h] if slot == 0 else ret_recv[h, slot]
            factor = jnp.exp2(st[h, slot, 0:1, :] - back[0:1])
            cd[h, 0:1, slot * ROWS : (slot + 1) * ROWS] = factor * back[1:2]
            rows = slice(slot * ROWS, (slot + 1) * ROWS)
            column = jnp.broadcast_to(factor, (ROWS, ROWS)).T
            dop[h, rows, :] = (do_all[h, rows, :].astype(F32) * column).astype(BF)

    def scores_back(h, chunks):
        for c in chunks:
            rows = slice(c * CHUNK, (c + 1) * CHUNK)
            value = kv_all[h, 1, rows, :]
            for pair in range(4):
                cols = slice(pair * CHUNK, (pair + 1) * CHUNK)
                dp = dot_nt(value, dop[h, cols, :])
                ds = p_scr[h, rows, cols].astype(F32) * (dp - cd[h, 0:1, cols])
                ds_scr[rows, cols] = ds.astype(BF)

    def keys_back(h, chunks):
        for c in chunks:
            rows = slice(c * CHUNK, (c + 1) * CHUNK)
            dkv_scr[h, rows, 0:HDIM] = dot_nn(ds_scr[rows, :], q_all[h]).astype(BF)
            dkv_scr[h, rows, HDIM : 2 * HDIM] = dot_nn(p_scr[h, rows, :], dop[h]).astype(BF)

    def queries_back(h):
        for pair in (3, 2, 1, 0):
            cols = slice(pair * CHUNK, (pair + 1) * CHUNK)
            dq = dot_nn(kt[h], ds_scr[:, cols])
            for i in range(2):
                dq_part[h, 2 * pair + i] = dq[:, i * ROWS : (i + 1) * ROWS].astype(BF)

    def dq_second(h):
        for n, off in enumerate((2, -2)):
            keys = [("mid", 3), ("mid", 4)] if off > 0 else [("mid", -3)]
            total = dq_part[h, SLOT[off]].astype(F32)
            for key in keys:
                total += dq_in[h, s_recv("dq", h, (dq_in,), key)].astype(F32)
            dq_mid[h, n] = total.astype(BF)
            s_send("dq", h, (dq_mid.at[h, n],), (dq_in,), -off, off)

    def dq_write(h, boxes):
        total = dq_part[h, 0].astype(F32)
        for i in boxes:
            total += dq_in[h, i].astype(F32)
        gq_ref[:, h * HDIM : (h + 1) * HDIM] = (total * SCALE).T.astype(BF)

    def dq_finish(h):
        dq_write(h, [s_recv("dq", h, (dq_in,), key) for key in (1, -1, 2, -2)])

    def dq_direct(h):
        for off in (4, 3, -3, 2, -2, 1, -1):
            i = SLOT[-off] - 1
            send(dq_part.at[h, SLOT[off]], dq_in.at[h, i], ("dq", 0, h, i), to_ctx=at_z(off))

    def dq_direct_finish(h):
        for i in range(NZ - 1):
            recv(dq_in.at[h, i], ("dq", 0, h, i))
        dq_write(h, range(NZ - 1))

    def keys_to_sibling(h):
        send(dkv_scr.at[h, pl.ds(SECT // 2, SECT // 2)], r1_sec.at[h], ("r1s", h), to_ctx=sibling)
        src = dkv_scr.at[h, pl.ds(SECT + HIST // 2, HIST // 2)]
        send(src, r1_hist.at[h], ("r1h", h), to_ctx=sibling)

    def keys_along_y(h):
        recv(r1_sec.at[h], ("r1s", h))
        recv(r1_hist.at[h], ("r1h", h))
        for dy in (2, 1, 3, 0):
            there = (NY - dy) % NY
            for name, got, total, into, start, size in (
                ("r2s", r1_sec, t_sec, r2_sec, 0, ROWS),
                ("r2h", r1_hist, t_hist, r2_hist, SECT, HCAP),
            ):
                rows = slice(dy * size, (dy + 1) * size)
                own = dkv_scr[h, start + dy * size : start + (dy + 1) * size, :].astype(F32)
                total[h, rows, :] = (own + got[h, rows, :].astype(F32)).astype(BF)
                if dy:
                    src = total.at[h, pl.ds(dy * size, size)]
                    send(src, into.at[h, there], (name, h, there), to_ctx=at_y(dy))

    def keys_finish(h):
        cols = slice(h * HDIM, (h + 1) * HDIM)
        for name, total, into, size, k_out, v_out in (
            ("r2s", t_sec, r2_sec, ROWS, gk_ref, gv_ref),
            ("r2h", t_hist, r2_hist, HCAP, ghk_ref, ghv_ref),
        ):
            value = total[h, 0:size, :].astype(F32)
            for dy in range(1, NY):
                recv(into.at[h, dy], (name, h, dy))
                value = value + into[h, dy].astype(F32)
            k_out[:, cols] = (value[:, 0:HDIM] * SCALE).astype(BF)
            v_out[:, cols] = value[:, HDIM : 2 * HDIM].astype(BF)

    def project():
        rows = jnp.concatenate(attn, axis=1)
        for dx in (2, 1, 3):
            there = (NX - dx) % NX
            po_send[dx] = dot_nn(rows, w_cols(dx)).astype(BF)
            send(po_send.at[dx], po_recv.at[there], ("po", there), to_head=at_x(dx))
        po_send[0] = dot_nn(rows, w_cols(0)).astype(BF)

    def project_finish():
        total = po_send[0].astype(F32)
        for dx in (1, 3, 2):
            recv(po_recv.at[dx], ("po", dx))
            total += po_recv[dx].astype(F32)
        out_ref[...] = total.astype(BF)

    o_first = functools.partial(s_first, "o", parts=o_parts, boxes=o_boxes)
    o_near = functools.partial(s_near, "o", parts=o_parts, boxes=o_boxes)
    dq_first = functools.partial(s_first, "dq", parts=(dq_part,), boxes=(dq_in,))
    dq_near = functools.partial(s_near, "dq", parts=(dq_part,), boxes=(dq_in,))

    z_second(q_all, "q", 0)
    kv_second(0)
    z_second(q_all, "q", 1)
    z_second(q_all, "q", 2)
    kv_rest(0)
    z_rest(q_all, "q", 0)
    forward(0, 3)
    forward(0, 2)
    o_first(0)
    kv_second(1)
    forward(0, 1)
    forward(0, 0)
    o_near(0)
    kv_second(2)
    cotangent()
    kv_rest(1)
    z_rest(q_all, "q", 1)
    forward(1, 3)
    forward(1, 2)
    o_first(1)
    o_second(0)
    forward(1, 1)
    z_second(do_all, "d", 0)
    forward(1, 0)
    o_near(1)
    z_second(do_all, "d", 1)
    kv_rest(2)
    z_rest(q_all, "q", 2)
    forward(2, 3)
    z_second(do_all, "d", 2)
    forward(2, 2)
    o_first(2)
    o_second(1)
    o_finish(0)
    forward(2, 1)
    forward(2, 0)
    o_near(2)
    z_rest(do_all, "d", 0)
    o_second(2)
    o_finish(1)
    settle(0)
    scores_back(0, (2, 3, 4))
    keys_back(0, (2, 3, 4))
    keys_to_sibling(0)
    o_finish(2)
    project()
    scores_back(0, (0, 1))
    queries_back(0)
    dq_first(0)
    dq_near(0)
    keys_back(0, (0, 1))
    z_rest(do_all, "d", 1)
    settle(1)
    keys_along_y(0)
    scores_back(1, (2, 3, 4))
    keys_back(1, (2, 3, 4))
    keys_to_sibling(1)
    dq_second(0)
    scores_back(1, (0, 1))
    queries_back(1)
    dq_first(1)
    dq_near(1)
    keys_back(1, (0, 1))
    z_rest(do_all, "d", 2)
    settle(2)
    keys_along_y(1)
    scores_back(2, (2, 3, 4))
    keys_back(2, (2, 3, 4))
    keys_to_sibling(2)
    dq_second(1)
    scores_back(2, (0, 1))
    queries_back(2)
    dq_direct(2)
    keys_back(2, (0, 1))
    keys_along_y(2)
    keys_finish(0)
    dq_finish(0)
    project_finish()
    keys_finish(1)
    dq_finish(1)
    keys_finish(2)
    dq_direct_finish(2)

    for copy in sent:
        copy.wait_send()
    assert len(sems.names) <= N_SEMS, len(sems.names)


def write_kernel(*refs):
    n = (len(refs) - 1) // 2
    sems = refs[-1]
    copies = [pltpu.make_async_copy(refs[i], refs[n + i], sems.at[i]) for i in range(n)]
    for copy in copies:
        copy.start()
    for copy in copies:
        copy.wait()


def write(arrays):
    n = len(arrays)
    return pl.pallas_call(
        write_kernel,
        out_shape=[jax.ShapeDtypeStruct(a.shape, a.dtype) for a in arrays],
        in_specs=[pl.BlockSpec(memory_space=pltpu.VMEM)] * n,
        out_specs=[pl.BlockSpec(memory_space=pl.ANY)] * n,
        scratch_shapes=[pltpu.SemaphoreType.DMA((n,))],
    )(*arrays)


def shards(sec_q, sec_k, sec_v, hist_k, hist_v, frame_levels, frame_counts, w_out, grad_out):
    vmem = pl.BlockSpec(memory_space=pltpu.VMEM)
    smem = pl.BlockSpec(memory_space=pltpu.SMEM)
    anywhere = pl.BlockSpec(memory_space=pl.ANY)
    box = (HEADS, NZ, HDIM, ROWS)
    mid = (HEADS, 2, HDIM, ROWS)
    scratch = [
        pltpu.VMEM((HEADS, QT, HDIM), BF),
        pltpu.VMEM((HEADS, 2, KT, HDIM), BF),
        pltpu.VMEM((HEADS, HDIM, KT), BF),
        pltpu.VMEM((HEADS, HDIM, KT), BF),
        pltpu.VMEM((WIDTH, NX * OCOLS), BF),
        pltpu.VMEM((NX, ROWS, OCOLS), BF),
        pltpu.VMEM((HEADS, QT, HDIM), BF),
        pltpu.VMEM((HEADS, QT, HDIM), BF),
        pltpu.VMEM((HIST, CHUNK), F32),
        pltpu.VMEM((KT, CHUNK), F32),
        pltpu.VMEM((HEADS, KT, QT), BF),
        pltpu.VMEM(box, BF),
        pltpu.VMEM((KT, QT), BF),
        pltpu.VMEM(box, BF),
        pltpu.VMEM((HEADS, KT, 2 * HDIM), BF),
        pltpu.VMEM((HEADS, NZ, 8, ROWS), F32),
        pltpu.VMEM((HEADS, 8, ROWS), F32),
        pltpu.VMEM((HEADS, NZ, 8, ROWS), F32),
        pltpu.VMEM((HEADS, 8, QT), F32),
        pltpu.VMEM(mid, BF),
        pltpu.VMEM(box, BF),
        pltpu.VMEM((HEADS, 2, 8, ROWS), F32),
        pltpu.VMEM((HEADS, NZ, 8, ROWS), F32),
        pltpu.VMEM(mid, BF),
        pltpu.VMEM(box, BF),
        pltpu.VMEM((HEADS, SECT // 2, 2 * HDIM), BF),
        pltpu.VMEM((HEADS, HIST // 2, 2 * HDIM), BF),
        pltpu.VMEM((HEADS, SECT // 2, 2 * HDIM), BF),
        pltpu.VMEM((HEADS, HIST // 2, 2 * HDIM), BF),
        pltpu.VMEM((HEADS, NY, ROWS, 2 * HDIM), BF),
        pltpu.VMEM((HEADS, NY, HCAP, 2 * HDIM), BF),
        pltpu.VMEM((NX, ROWS, OCOLS), BF),
        pltpu.VMEM((NX, ROWS, OCOLS), BF),
        pltpu.SemaphoreType.DMA((N_SEMS,)),
        pltpu.SemaphoreType.DMA((N_SEMS,)),
        pltpu.SemaphoreType.DMA(()),
    ]
    shapes = [
        jax.ShapeDtypeStruct((ROWS, OCOLS), BF),
        jax.ShapeDtypeStruct((ROWS, WIDTH), BF),
        jax.ShapeDtypeStruct((ROWS, WIDTH), BF),
        jax.ShapeDtypeStruct((ROWS, WIDTH), BF),
        jax.ShapeDtypeStruct((HCAP, WIDTH), BF),
        jax.ShapeDtypeStruct((HCAP, WIDTH), BF),
    ]
    results = pl.pallas_call(
        kernel,
        out_shape=shapes,
        in_specs=[vmem] * 5 + [smem] * 2 + [anywhere, vmem],
        out_specs=[vmem] * 6,
        scratch_shapes=scratch,
        compiler_params=pltpu.CompilerParams(
            collective_id=0, has_side_effects=True, vmem_limit_bytes=60 * 1024 * 1024
        ),
    )(sec_q, sec_k, sec_v, hist_k, hist_v, frame_levels.T, frame_counts, w_out, grad_out)
    return write(results)


def solution(mesh):
    both = P("ctx", "head")
    placed = (both, both, both, both, both, P(), P(), P("head", None), both)
    return jax.shard_map(
        shards, mesh=mesh, in_specs=placed, out_specs=(both,) * 6, check_vma=False
    )
```

time: 102 us -> 76.2 us (0.75)
  the two profiles are of different devices: /device:TPU:38 before, /device:TPU:1 now
where the time goes in v2:
time: 76.2 us; the launch traced here: 74.9 us
  Pallas kernels  74.1 us (97%)
  between operations  0.8 us (1%)
    pallas_call x1, Pallas kernels, shards(): pl.pallas_call(kernel, out_shape=shapes, in_specs=[vmem] * 5 + [smem] * 2...  72.1 us
    pallas_call x1, Pallas kernels, write(): pl.pallas_call(write_kernel, out_shape=[jax.ShapeDtypeStruct(a.shape, a.d...  1.92 us

profile of v2, /device:TPU:1, one launch (start us, length us, event | category | flops | bytes accessed | tf_op | source)
XLA Modules:
  0.0 74.9 jit_solution(3120546902624196885)
XLA Ops:
  0.6 72.1 %shard_map.136 = (bf16[128,768]{1,0:T(8,128)(2,1)}, bf16[128,384]{1,0:T(8,128)(2,1)}, bf16[128,384]{1,0:T(8,128)(2,1)}, bf16[128,384]{1,0:T(8,128)(2,1)}, bf16[3...) custom-call(bf16[128,384]{1,0:T(8,128)(2,1)} %q_ref.1, bf16[128,384]{1,0:T(8,128)(2,1)} %k_ref.1, bf16[128,384]{1,0:T(8,128)(2,1)} %v_ref.1, ...), custom_call_target="tpu_custom_call" | custom-call | tf_op jit(solution)/shard_map/pallas_call | solution.py:587
  72.8 1.9 %shard_map.137 = (bf16[128,768]{1,0:T(8,128)(2,1)}, bf16[128,384]{1,0:T(8,128)(2,1)}, bf16[128,384]{1,0:T(8,128)(2,1)}, bf16[128,384]{1,0:T(8,128)(2,1)}, bf16[3...) custom-call(bf16[128,768]{1,0:T(8,128)(2,1)} %get-tuple-element.12.refs_0_, bf16[128,384]{1,0:T(8,128)(2,1)} %get-tuple-element.13.refs_1_, ...), custom_call_target="tpu_custom_call" | custom-call | tf_op jit(solution)/shard_map/pallas_call | solution.py:526

commit v3 on v2

--- a/solution.py
+++ b/solution.py
@@ -33,6 +33,24 @@
 SLOT = {off: i for i, off in enumerate(OFFS)}
 SLOT[-4] = SLOT[4]
 
+DIRECT = {o: o for o in OFFS[1:]}
+TWO = {4: 2, 3: 1, -3: -1, 2: 2, -2: -2, 1: 1, -1: -1}
+THREE = {4: 2, 3: 1, -3: -1, 2: 1, -2: -1, 1: 1, -1: -1}
+RING = {4: 1, 3: 1, -3: -1, 2: 1, -2: -1, 1: 1, -1: -1}
+
+
+def feeders(route, off):
+    return [o for o in OFFS[1:] if o - route[o] == off]
+
+
+def depth(route, off):
+    return 0 if off == 0 else 1 + depth(route, off - route[off])
+
+
+def layer(route, n):
+    return [o for o in OFFS if depth(route, o) == n]
+
+
 SCALE = 1.0 / math.sqrt(HDIM)
 SCALE2 = SCALE * math.log2(math.e)
 
@@ -53,7 +71,10 @@
         return self.names.setdefault(name, len(self.names))
 
 
-N_SEMS = 224
+N_SEMS = 256
+Q_ROUTE, D_ROUTE = TWO, THREE
+O_ROUTE = (TWO, TWO, TWO)
+DQ_ROUTE = (DIRECT, TWO, TWO)
 
 
 def kernel(
@@ -64,7 +85,7 @@
     st, ret, ret_recv, cd,
     o_mid, o_in, st_mid, st_in, dq_mid, dq_in,
     r1_sec, r1_hist, t_sec, t_hist, r2_sec, r2_hist,
-    po_send, po_recv,
+    at_all, w_far, acc,
     send_sem, recv_sem, w_sem,
 ):
     ctx = lax.axis_index("ctx")
@@ -128,26 +149,24 @@
     def z_slot(buf, h, off):
         return buf.at[h, pl.ds(SLOT[off] * ROWS, ROWS), :]
 
-    def z_send(buf, tag, h, off, there, to):
-        send(z_slot(buf, h, off), z_slot(buf, h, there), (tag, h, there), to_ctx=at_z(to))
-
-    def z_recv(buf, tag, h, *offs):
-        for off in offs:
-            recv(z_slot(buf, h, off), (tag, h, off))
-
-    def z_first(buf, tag, h):
-        for off in (2, -2, 1, -1):
-            z_send(buf, tag, h, 0, -off, off)
-
-    def z_second(buf, tag, h):
-        z_recv(buf, tag, h, 2)
-        z_send(buf, tag, h, 2, 4, -2)
-        z_send(buf, tag, h, 2, 3, -1)
-        z_recv(buf, tag, h, -2)
-        z_send(buf, tag, h, -2, -3, 1)
-
-    def z_rest(buf, tag, h):
-        z_recv(buf, tag, h, 1, -1, 3, -3, 4)
+    bufs = {"q": (q_all, Q_ROUTE), "d": (do_all, D_ROUTE)}
+
+    def gather(tag, h, n):
+        buf, route = bufs[tag]
+        for o in layer(route, n):
+            if not feeders(route, o):
+                continue
+            if o:
+                recv(z_slot(buf, h, o), (tag, h, o))
+            for off in feeders(route, o):
+                dst = z_slot(buf, h, off)
+                send(z_slot(buf, h, o), dst, (tag, h, off), to_ctx=at_z(-route[off]))
+
+    def gather_rest(tag, h):
+        buf, route = bufs[tag]
+        for o in OFFS[1:]:
+            if not feeders(route, o):
+                recv(z_slot(buf, h, o), (tag, h, o))
 
     pieces = ((0, ROWS), (SECT, HCAP))
 
@@ -182,7 +201,7 @@
         send(g_ref, g_all.at[there], ("g", there), to_head=at_x(dx))
     for h in range(HEADS):
         kv_first(h)
-        z_first(q_all, "q", h)
+        gather("q", h, 0)
 
     row = lax.broadcasted_iota(jnp.int32, (HIST, CHUNK), 0)
     limit = jnp.zeros((HIST, CHUNK), jnp.int32)
@@ -210,7 +229,6 @@
             d_attn += dot_nt(g_all[dx], w_cols(dx))
         for h in range(HEADS):
             do_all[h, 0:ROWS, :] = d_attn[:, h * HDIM : (h + 1) * HDIM].astype(BF)
-            z_first(do_all, "d", h)
 
     def forward(h, pair):
         cols = slice(pair * CHUNK, (pair + 1) * CHUNK)
@@ -240,32 +258,19 @@
             st[h, slot, 0:1, :] = top[:, half]
             st[h, slot, 1:2, :] = total[:, half]
 
-    INBOX = {("mid", 3): 0, ("mid", -3): 1, ("mid", 4): 2, 1: 3, -1: 4, 2: 5, -2: 6}
-
-    def s_send(tag, h, srcs, boxes, key, to):
-        i = INBOX[key]
+    def s_send(tag, h, off, srcs, boxes, route):
+        i = SLOT[off] - 1
         for n, (src, box) in enumerate(zip(srcs, boxes)):
-            send(src, box.at[h, i], (tag, n, h, i), to_ctx=at_z(to))
-
-    def s_recv(tag, h, boxes, key):
-        i = INBOX[key]
+            send(src, box.at[h, i], (tag, n, h, i), to_ctx=at_z(route[off]))
+
+    def s_recv(tag, h, off, boxes):
+        i = SLOT[off] - 1
         for n, box in enumerate(boxes):
             recv(box.at[h, i], (tag, n, h, i))
         return i
 
-    def s_first(tag, h, parts, boxes):
-        def at(off):
-            return [p.at[h, SLOT[off]] for p in parts]
-
-        s_send(tag, h, at(4), boxes, ("mid", 4), 2)
-        s_send(tag, h, at(3), boxes, ("mid", 3), 1)
-        s_send(tag, h, at(-3), boxes, ("mid", -3), -1)
-
-    def s_near(tag, h, parts, boxes):
-        for off in (1, -1):
-            s_send(tag, h, [p.at[h, SLOT[off]] for p in parts], boxes, -off, off)
-
-    o_parts, o_boxes = (o_part, st), (o_in, st_in)
+    def stage(route, n):
+        return layer(route, max(depth(route, o) for o in OFFS) + 1 - n)
 
     def merge(terms):
         peak = functools.reduce(jnp.maximum, [t[0] for t in terms])
@@ -277,28 +282,33 @@
     def o_triple(h, slot):
         return st[h, slot, 0:1, :], st[h, slot, 1:2, :], o_part[h, slot].astype(F32)
 
-    def o_arrived(h, key):
-        i = s_recv("o", h, o_boxes, key)
+    def o_arrived(h, off):
+        i = s_recv("o", h, off, (o_in, st_in))
         return st_in[h, i, 0:1, :], st_in[h, i, 1:2, :], o_in[h, i].astype(F32)
 
-    def o_second(h):
-        for n, off in enumerate((2, -2)):
-            terms = [o_triple(h, SLOT[off]), o_arrived(h, ("mid", 3 if off > 0 else -3))]
-            if off > 0:
-                terms.append(o_arrived(h, ("mid", 4)))
-            peak, whole, product = merge(terms)
-            st_mid[h, n, 0:1, :] = peak
-            st_mid[h, n, 1:2, :] = whole
-            o_mid[h, n] = product.astype(BF)
-            s_send("o", h, (o_mid.at[h, n], st_mid.at[h, n]), o_boxes, -off, off)
-
-    attn = []
+    def o_stage(h, n):
+        route = O_ROUTE[h]
+        for off in stage(route, n):
+            slot = SLOT[off]
+            srcs = (o_part.at[h, slot], st.at[h, slot])
+            before = feeders(route, off)
+            if before:
+                terms = [o_triple(h, slot)] + [o_arrived(h, o) for o in before]
+                peak, whole, product = merge(terms)
+                st_mid[h, slot, 0:1, :] = peak
+                st_mid[h, slot, 1:2, :] = whole
+                o_mid[h, slot] = product.astype(BF)
+                srcs = (o_mid.at[h, slot], st_mid.at[h, slot])
+            s_send("o", h, off, srcs, (o_in, st_in), route)
 
     def o_finish(h):
-        terms = [o_triple(h, 0)] + [o_arrived(h, key) for key in (1, -1, 2, -2)]
+        terms = [o_triple(h, 0)] + [o_arrived(h, o) for o in feeders(O_ROUTE[h], 0)]
         peak, whole, product = merge(terms)
         mine = (product / whole).T.astype(BF)
-        attn.append(mine)
+        at_all[h, 0] = mine
+        for dx in (2, 1, 3):
+            there = (NX - dx) % NX
+            send(at_all.at[h, 0], at_all.at[h, there], ("at", h, there), to_head=at_x(dx))
         both = mine.astype(F32) * do_all[h, 0:ROWS, :].astype(F32)
         delta = jnp.sum(both.T, axis=0, keepdims=True)
         ret[h, 0:1, :] = peak + jnp.log2(whole)
@@ -341,33 +351,25 @@
             for i in range(2):
                 dq_part[h, 2 * pair + i] = dq[:, i * ROWS : (i + 1) * ROWS].astype(BF)
 
-    def dq_second(h):
-        for n, off in enumerate((2, -2)):
-            keys = [("mid", 3), ("mid", 4)] if off > 0 else [("mid", -3)]
-            total = dq_part[h, SLOT[off]].astype(F32)
-            for key in keys:
-                total += dq_in[h, s_recv("dq", h, (dq_in,), key)].astype(F32)
-            dq_mid[h, n] = total.astype(BF)
-            s_send("dq", h, (dq_mid.at[h, n],), (dq_in,), -off, off)
-
-    def dq_write(h, boxes):
+    def dq_stage(h, n):
+        route = DQ_ROUTE[h]
+        for off in stage(route, n):
+            slot = SLOT[off]
+            src = dq_part.at[h, slot]
+            before = feeders(route, off)
+            if before:
+                total = dq_part[h, slot].astype(F32)
+                for o in before:
+                    total += dq_in[h, s_recv("dq", h, o, (dq_in,))].astype(F32)
+                dq_mid[h, slot] = total.astype(BF)
+                src = dq_mid.at[h, slot]
+            s_send("dq", h, off, (src,), (dq_in,), route)
+
+    def dq_finish(h):
         total = dq_part[h, 0].astype(F32)
-        for i in boxes:
-            total += dq_in[h, i].astype(F32)
+        for o in feeders(DQ_ROUTE[h], 0):
+            total += dq_in[h, s_recv("dq", h, o, (dq_in,))].astype(F32)
         gq_ref[:, h * HDIM : (h + 1) * HDIM] = (total * SCALE).T.astype(BF)
-
-    def dq_finish(h):
-        dq_write(h, [s_recv("dq", h, (dq_in,), key) for key in (1, -1, 2, -2)])
-
-    def dq_direct(h):
-        for off in (4, 3, -3, 2, -2, 1, -1):
-            i = SLOT[-off] - 1
-            send(dq_part.at[h, SLOT[off]], dq_in.at[h, i], ("dq", 0, h, i), to_ctx=at_z(off))
-
-    def dq_direct_finish(h):
-        for i in range(NZ - 1):
-            recv(dq_in.at[h, i], ("dq", 0, h, i))
-        dq_write(h, range(NZ - 1))
 
     def keys_to_sibling(h):
         send(dkv_scr.at[h, pl.ds(SECT // 2, SECT // 2)], r1_sec.at[h], ("r1s", h), to_ctx=sibling)
@@ -403,108 +405,125 @@
             k_out[:, cols] = (value[:, 0:HDIM] * SCALE).astype(BF)
             v_out[:, cols] = value[:, HDIM : 2 * HDIM].astype(BF)
 
-    def project():
-        rows = jnp.concatenate(attn, axis=1)
+    def half(base):
+        return pl.ds(pl.multiple_of(base + core * (OCOLS // 2), OCOLS // 2), OCOLS // 2)
+
+    def w_first():
         for dx in (2, 1, 3):
             there = (NX - dx) % NX
-            po_send[dx] = dot_nn(rows, w_cols(dx)).astype(BF)
-            send(po_send.at[dx], po_recv.at[there], ("po", there), to_head=at_x(dx))
-        po_send[0] = dot_nn(rows, w_cols(0)).astype(BF)
-
-    def project_finish():
-        total = po_send[0].astype(F32)
+            src = w_all.at[:, half(at_x(dx) * OCOLS)]
+            send(src, w_far.at[there, :, half(0)], ("w", there), to_head=at_x(dx))
+
+    def w_second():
         for dx in (1, 3, 2):
-            recv(po_recv.at[dx], ("po", dx))
-            total += po_recv[dx].astype(F32)
-        out_ref[...] = total.astype(BF)
-
-    o_first = functools.partial(s_first, "o", parts=o_parts, boxes=o_boxes)
-    o_near = functools.partial(s_near, "o", parts=o_parts, boxes=o_boxes)
-    dq_first = functools.partial(s_first, "dq", parts=(dq_part,), boxes=(dq_in,))
-    dq_near = functools.partial(s_near, "dq", parts=(dq_part,), boxes=(dq_in,))
-
-    z_second(q_all, "q", 0)
+            recv(w_far.at[dx, :, half(0)], ("w", dx))
+            send(w_far.at[dx, :, half(0)], w_far.at[dx, :, half(0)], ("ws", dx), to_ctx=sibling)
+
+    def w_rest():
+        for dx in (1, 3, 2):
+            recv(w_far.at[dx, :, half(0)], ("ws", dx))
+
+    def project(heads, first, last):
+        rows = slice(heads[0] * HDIM, (heads[-1] + 1) * HDIM)
+        total = None if first else acc[...]
+        for dx in (0, 1, 3, 2):
+            if dx:
+                for h in heads:
+                    recv(at_all.at[h, dx], ("at", h, dx))
+            left = jnp.concatenate([at_all[h, dx] for h in heads], axis=1)
+            part = dot_nn(left, w_far[dx, rows, :] if dx else w_cols(0)[rows, :])
+            total = part if total is None else total + part
+        if last:
+            out_ref[...] = total.astype(BF)
+        else:
+            acc[...] = total
+
+    gather("q", 0, 1)
     kv_second(0)
-    z_second(q_all, "q", 1)
-    z_second(q_all, "q", 2)
+    gather("q", 1, 1)
+    gather("q", 2, 1)
     kv_rest(0)
-    z_rest(q_all, "q", 0)
+    kv_second(1)
+    gather_rest("q", 0)
+    forward(0, 2)
+    cotangent()
+    gather("d", 0, 0)
+    gather("d", 1, 0)
     forward(0, 3)
-    forward(0, 2)
-    o_first(0)
-    kv_second(1)
+    kv_second(2)
+    kv_rest(1)
+    o_stage(0, 1)
+    gather_rest("q", 1)
+    forward(1, 2)
+    gather("d", 2, 0)
+    forward(1, 3)
+    gather_rest("q", 2)
+    kv_rest(2)
+    gather("d", 0, 1)
+    o_stage(1, 1)
+    w_first()
     forward(0, 1)
     forward(0, 0)
-    o_near(0)
-    kv_second(2)
-    cotangent()
-    kv_rest(1)
-    z_rest(q_all, "q", 1)
-    forward(1, 3)
-    forward(1, 2)
-    o_first(1)
-    o_second(0)
+    o_stage(0, 2)
+    gather("d", 1, 1)
     forward(1, 1)
-    z_second(do_all, "d", 0)
+    forward(2, 3)
+    gather("d", 2, 1)
+    forward(2, 2)
+    gather("d", 0, 2)
+    o_stage(2, 1)
+    forward(2, 0)
+    forward(2, 1)
     forward(1, 0)
-    o_near(1)
-    z_second(do_all, "d", 1)
-    kv_rest(2)
-    z_rest(q_all, "q", 2)
-    forward(2, 3)
-    z_second(do_all, "d", 2)
-    forward(2, 2)
-    o_first(2)
-    o_second(1)
     o_finish(0)
-    forward(2, 1)
-    forward(2, 0)
-    o_near(2)
-    z_rest(do_all, "d", 0)
-    o_second(2)
+    o_stage(1, 2)
+    o_stage(2, 2)
+    gather("d", 1, 2)
+    gather_rest("d", 0)
+    settle(0)
+    scores_back(0, (0, 1))
     o_finish(1)
-    settle(0)
+    gather("d", 2, 2)
     scores_back(0, (2, 3, 4))
     keys_back(0, (2, 3, 4))
     keys_to_sibling(0)
     o_finish(2)
-    project()
-    scores_back(0, (0, 1))
     queries_back(0)
-    dq_first(0)
-    dq_near(0)
+    dq_stage(0, 1)
+    w_second()
     keys_back(0, (0, 1))
-    z_rest(do_all, "d", 1)
+    gather_rest("d", 1)
+    keys_along_y(0)
     settle(1)
-    keys_along_y(0)
+    scores_back(1, (0, 1))
+    keys_back(1, (0, 1))
     scores_back(1, (2, 3, 4))
     keys_back(1, (2, 3, 4))
+    gather_rest("d", 2)
+    queries_back(1)
     keys_to_sibling(1)
-    dq_second(0)
-    scores_back(1, (0, 1))
-    queries_back(1)
-    dq_first(1)
-    dq_near(1)
-    keys_back(1, (0, 1))
-    z_rest(do_all, "d", 2)
+    dq_stage(1, 1)
     settle(2)
+    scores_back(2, (0, 1))
+    scores_back(2, (2, 3, 4))
     keys_along_y(1)
-    scores_back(2, (2, 3, 4))
+    queries_back(2)
+    dq_stage(2, 1)
     keys_back(2, (2, 3, 4))
     keys_to_sibling(2)
-    dq_second(1)
-    scores_back(2, (0, 1))
-    queries_back(2)
-    dq_direct(2)
     keys_back(2, (0, 1))
+    dq_stage(1, 2)
     keys_along_y(2)
+    dq_stage(2, 2)
+    w_rest()
+    dq_finish(0)
+    keys_finish(1)
+    project((0, 1), True, False)
     keys_finish(0)
-    dq_finish(0)
-    project_finish()
-    keys_finish(1)
+    project((2,), False, True)
     dq_finish(1)
     keys_finish(2)
-    dq_direct_finish(2)
+    dq_finish(2)
 
     for copy in sent:
         copy.wait_send()
@@ -537,7 +556,6 @@
     smem = pl.BlockSpec(memory_space=pltpu.SMEM)
     anywhere = pl.BlockSpec(memory_space=pl.ANY)
     box = (HEADS, NZ, HDIM, ROWS)
-    mid = (HEADS, 2, HDIM, ROWS)
     scratch = [
         pltpu.VMEM((HEADS, QT, HDIM), BF),
         pltpu.VMEM((HEADS, 2, KT, HDIM), BF),
@@ -554,15 +572,15 @@
         pltpu.VMEM((KT, QT), BF),
         pltpu.VMEM(box, BF),
         pltpu.VMEM((HEADS, KT, 2 * HDIM), BF),
-        pltpu.VMEM((HEADS, NZ, 8, ROWS), F32),
-        pltpu.VMEM((HEADS, 8, ROWS), F32),
-        pltpu.VMEM((HEADS, NZ, 8, ROWS), F32),
+        pltpu.VMEM((HEADS, NZ, 2, ROWS), F32),
+        pltpu.VMEM((HEADS, 2, ROWS), F32),
+        pltpu.VMEM((HEADS, NZ, 2, ROWS), F32),
         pltpu.VMEM((HEADS, 8, QT), F32),
-        pltpu.VMEM(mid, BF),
         pltpu.VMEM(box, BF),
-        pltpu.VMEM((HEADS, 2, 8, ROWS), F32),
-        pltpu.VMEM((HEADS, NZ, 8, ROWS), F32),
-        pltpu.VMEM(mid, BF),
+        pltpu.VMEM(box, BF),
+        pltpu.VMEM((HEADS, NZ, 2, ROWS), F32),
+        pltpu.VMEM((HEADS, NZ, 2, ROWS), F32),
+        pltpu.VMEM(box, BF),
         pltpu.VMEM(box, BF),
         pltpu.VMEM((HEADS, SECT // 2, 2 * HDIM), BF),
         pltpu.VMEM((HEADS, HIST // 2, 2 * HDIM), BF),
@@ -570,8 +588,9 @@
         pltpu.VMEM((HEADS, HIST // 2, 2 * HDIM), BF),
         pltpu.VMEM((HEADS, NY, ROWS, 2 * HDIM), BF),
         pltpu.VMEM((HEADS, NY, HCAP, 2 * HDIM), BF),
-        pltpu.VMEM((NX, ROWS, OCOLS), BF),
-        pltpu.VMEM((NX, ROWS, OCOLS), BF),
+        pltpu.VMEM((HEADS, NX, ROWS, HDIM), BF),
+        pltpu.VMEM((NX, WIDTH, OCOLS), BF),
+        pltpu.VMEM((ROWS, OCOLS), F32),
         pltpu.SemaphoreType.DMA((N_SEMS,)),
         pltpu.SemaphoreType.DMA((N_SEMS,)),
         pltpu.SemaphoreType.DMA(()),

time: 76.2 us -> 69.3 us (0.909); the launches traced: 74.9 us -> 69.2 us
  Pallas kernels: 74.1 us -> 68.4 us
    pallas_call x1, Pallas kernels: 72.1 us -> 66.5 us  [shards(): pl.pallas_call(kernel, out_shape=shapes, in_specs=[vmem] * 5 + [smem] * 2...]
where the time goes in v3:
time: 69.3 us; the launch traced here: 69.2 us
  Pallas kernels  68.4 us (99%)
  between operations  0.8 us (1%)
    pallas_call x1, Pallas kernels, shards(): pl.pallas_call(kernel, out_shape=shapes, in_specs=[vmem] * 5 + [smem] * 2...  66.5 us
    pallas_call x1, Pallas kernels, write(): pl.pallas_call(write_kernel, out_shape=[jax.ShapeDtypeStruct(a.shape, a.d...  1.92 us

profile of v3, /device:TPU:1, one launch (start us, length us, event | category | flops | bytes accessed | tf_op | source)
XLA Modules:
  0.0 69.2 jit_solution(8662977443037918357)
XLA Ops:
  0.6 66.5 %shard_map.136 = (bf16[128,768]{1,0:T(8,128)(2,1)}, bf16[128,384]{1,0:T(8,128)(2,1)}, bf16[128,384]{1,0:T(8,128)(2,1)}, bf16[128,384]{1,0:T(8,128)(2,1)}, bf16[3...) custom-call(bf16[128,384]{1,0:T(8,128)(2,1)} %q_ref.1, bf16[128,384]{1,0:T(8,128)(2,1)} %k_ref.1, bf16[128,384]{1,0:T(8,128)(2,1)} %v_ref.1, ...), custom_call_target="tpu_custom_call" | custom-call | tf_op jit(solution)/shard_map/pallas_call | solution.py:606
  67.1 1.9 %shard_map.137 = (bf16[128,768]{1,0:T(8,128)(2,1)}, bf16[128,384]{1,0:T(8,128)(2,1)}, bf16[128,384]{1,0:T(8,128)(2,1)}, bf16[128,384]{1,0:T(8,128)(2,1)}, bf16[3...) custom-call(bf16[128,768]{1,0:T(8,128)(2,1)} %get-tuple-element.12.refs_0_, bf16[128,384]{1,0:T(8,128)(2,1)} %get-tuple-element.13.refs_1_, ...), custom_call_target="tpu_custom_call" | custom-call | tf_op jit(solution)/shard_map/pallas_call | solution.py:545

commit v4 on v3

--- a/solution.py
+++ b/solution.py
@@ -71,7 +71,7 @@
         return self.names.setdefault(name, len(self.names))
 
 
-N_SEMS = 256
+N_SEND, N_RECV = 16, 88
 Q_ROUTE, D_ROUTE = TWO, THREE
 O_ROUTE = (TWO, TWO, TWO)
 DQ_ROUTE = (DIRECT, TWO, TWO)
@@ -106,25 +106,21 @@
 
     sibling = (z * NY + y) * NC + (1 - core)
 
-    sems = Sems()
-    sent = []
-
-    def send(src, dst, name, to_ctx=None, to_head=None):
-        i = sems(*name)
-        copy = pltpu.make_async_remote_copy(
-            src_ref=src, dst_ref=dst, send_sem=send_sem.at[i], recv_sem=recv_sem.at[i],
+    groups, arrivals = Sems(), Sems()
+
+    def remote(src, dst, group, key, to_ctx, to_head):
+        return pltpu.make_async_remote_copy(
+            src_ref=src, dst_ref=dst,
+            send_sem=send_sem.at[groups(group)], recv_sem=recv_sem.at[arrivals(*key)],
             device_id=(ctx if to_ctx is None else to_ctx, x if to_head is None else to_head),
             device_id_type=MESH,
         )
-        copy.start()
-        sent.append(copy)
-
-    def recv(dst, name):
-        i = sems(*name)
-        pltpu.make_async_remote_copy(
-            src_ref=dst, dst_ref=dst, send_sem=send_sem.at[i], recv_sem=recv_sem.at[i],
-            device_id=(sibling, x), device_id_type=MESH,
-        ).wait_recv()
+
+    def send(src, dst, group, key, to_ctx=None, to_head=None):
+        remote(src, dst, group, key, to_ctx, to_head).start()
+
+    def recv(same_size, group, key):
+        remote(same_size, same_size, group, key, sibling, None).wait_recv()
 
     barrier = pltpu.get_barrier_semaphore()
     peers = [(at_z(o), x) for o in OFFS[1:]]
@@ -157,16 +153,16 @@
             if not feeders(route, o):
                 continue
             if o:
-                recv(z_slot(buf, h, o), (tag, h, o))
+                recv(z_slot(buf, h, o), tag, (tag, h, o))
             for off in feeders(route, o):
+                key = (tag, h, off if feeders(route, off) else "rest")
                 dst = z_slot(buf, h, off)
-                send(z_slot(buf, h, o), dst, (tag, h, off), to_ctx=at_z(-route[off]))
+                send(z_slot(buf, h, o), dst, tag, key, to_ctx=at_z(-route[off]))
 
     def gather_rest(tag, h):
         buf, route = bufs[tag]
-        for o in OFFS[1:]:
-            if not feeders(route, o):
-                recv(z_slot(buf, h, o), (tag, h, o))
+        ends = [o for o in OFFS[1:] if not feeders(route, o)]
+        recv(buf.at[h, pl.ds(0, len(ends) * ROWS), :], tag, (tag, h, "rest"))
 
     pieces = ((0, ROWS), (SECT, HCAP))
 
@@ -176,21 +172,17 @@
             for start, size in pieces:
                 src = kv_all.at[h, :, pl.ds(start, size), :]
                 dst = kv_all.at[h, :, pl.ds(start + there * size, size), :]
-                send(src, dst, ("kv", h, there, start), to_ctx=at_y(dy))
+                send(src, dst, "kv", ("kv", h), to_ctx=at_y(dy))
 
     def kv_second(h):
-        for dy in (1, 3, 2):
-            for start, size in pieces:
-                recv(kv_all.at[h, :, pl.ds(start + dy * size, size), :], ("kv", h, dy, start))
+        recv(kv_all.at[h, :, pl.ds(0, (NY - 1) * (ROWS + HCAP)), :], "kv", ("kv", h))
         for start, size in pieces:
             src = kv_all.at[h, :, pl.ds(start, NY * size), :]
             dst = kv_all.at[h, :, pl.ds(start + NY * size, NY * size), :]
-            send(src, dst, ("kv", h, "sib", start), to_ctx=sibling)
+            send(src, dst, "kvs", ("kvs", h), to_ctx=sibling)
 
     def kv_rest(h):
-        for start, size in pieces:
-            dst = kv_all.at[h, :, pl.ds(start + NY * size, NY * size), :]
-            recv(dst, ("kv", h, "sib", start))
+        recv(kv_all.at[h, :, pl.ds(0, NY * (ROWS + HCAP)), :], "kvs", ("kvs", h))
         for i in range(KT // HDIM):
             rows = slice(i * HDIM, (i + 1) * HDIM)
             kt[h, :, rows] = kv_all[h, 0, rows, :].T
@@ -198,7 +190,7 @@
 
     for dx in (2, 1, 3):
         there = (NX - dx) % NX
-        send(g_ref, g_all.at[there], ("g", there), to_head=at_x(dx))
+        send(g_ref, g_all.at[there], "g", ("g", there), to_head=at_x(dx))
     for h in range(HEADS):
         kv_first(h)
         gather("q", h, 0)
@@ -225,7 +217,7 @@
         w_copy.wait()
         d_attn = dot_nt(g_ref[...], w_cols(0))
         for dx in (1, 3, 2):
-            recv(g_all.at[dx], ("g", dx))
+            recv(g_all.at[dx], "g", ("g", dx))
             d_attn += dot_nt(g_all[dx], w_cols(dx))
         for h in range(HEADS):
             do_all[h, 0:ROWS, :] = d_attn[:, h * HDIM : (h + 1) * HDIM].astype(BF)
@@ -260,14 +252,15 @@
 
     def s_send(tag, h, off, srcs, boxes, route):
         i = SLOT[off] - 1
+        key = (tag, h, off - route[off])
         for n, (src, box) in enumerate(zip(srcs, boxes)):
-            send(src, box.at[h, i], (tag, n, h, i), to_ctx=at_z(route[off]))
-
-    def s_recv(tag, h, off, boxes):
-        i = SLOT[off] - 1
+            send(src, box.at[h, i], (tag, n), key + (n,), to_ctx=at_z(route[off]))
+
+    def s_recv(tag, h, off, boxes, route):
+        before = feeders(route, off)
         for n, box in enumerate(boxes):
-            recv(box.at[h, i], (tag, n, h, i))
-        return i
+            recv(box.at[h, pl.ds(0, len(before))], (tag, n), (tag, h, off, n))
+        return [SLOT[o] - 1 for o in before]
 
     def stage(route, n):
         return layer(route, max(depth(route, o) for o in OFFS) + 1 - n)
@@ -283,18 +276,16 @@
         return st[h, slot, 0:1, :], st[h, slot, 1:2, :], o_part[h, slot].astype(F32)
 
     def o_arrived(h, off):
-        i = s_recv("o", h, off, (o_in, st_in))
-        return st_in[h, i, 0:1, :], st_in[h, i, 1:2, :], o_in[h, i].astype(F32)
+        boxes = s_recv("o", h, off, (o_in, st_in), O_ROUTE[h])
+        return [(st_in[h, i, 0:1, :], st_in[h, i, 1:2, :], o_in[h, i].astype(F32)) for i in boxes]
 
     def o_stage(h, n):
         route = O_ROUTE[h]
         for off in stage(route, n):
             slot = SLOT[off]
             srcs = (o_part.at[h, slot], st.at[h, slot])
-            before = feeders(route, off)
-            if before:
-                terms = [o_triple(h, slot)] + [o_arrived(h, o) for o in before]
-                peak, whole, product = merge(terms)
+            if feeders(route, off):
+                peak, whole, product = merge([o_triple(h, slot)] + o_arrived(h, off))
                 st_mid[h, slot, 0:1, :] = peak
                 st_mid[h, slot, 1:2, :] = whole
                 o_mid[h, slot] = product.astype(BF)
@@ -302,25 +293,23 @@
             s_send("o", h, off, srcs, (o_in, st_in), route)
 
     def o_finish(h):
-        terms = [o_triple(h, 0)] + [o_arrived(h, o) for o in feeders(O_ROUTE[h], 0)]
-        peak, whole, product = merge(terms)
+        peak, whole, product = merge([o_triple(h, 0)] + o_arrived(h, 0))
         mine = (product / whole).T.astype(BF)
         at_all[h, 0] = mine
         for dx in (2, 1, 3):
             there = (NX - dx) % NX
-            send(at_all.at[h, 0], at_all.at[h, there], ("at", h, there), to_head=at_x(dx))
+            send(at_all.at[h, 0], at_all.at[h, there], "at", ("at", h), to_head=at_x(dx))
         both = mine.astype(F32) * do_all[h, 0:ROWS, :].astype(F32)
         delta = jnp.sum(both.T, axis=0, keepdims=True)
         ret[h, 0:1, :] = peak + jnp.log2(whole)
         ret[h, 1:2, :] = delta
         for off in OFFS[1:]:
             there = SLOT[-off]
-            send(ret.at[h], ret_recv.at[h, there], ("ret", h, there), to_ctx=at_z(off))
+            send(ret.at[h], ret_recv.at[h, there], "ret", ("ret", h), to_ctx=at_z(off))
 
     def settle(h):
-        for slot in (0, 1, 2, 3, 4, 5, 6, 7):
-            if slot:
-                recv(ret_recv.at[h, slot], ("ret", h, slot))
+        recv(ret_recv.at[h, pl.ds(1, NZ - 1)], "ret", ("ret", h))
+        for slot in range(NZ):
             back = ret[h] if slot == 0 else ret_recv[h, slot]
             factor = jnp.exp2(st[h, slot, 0:1, :] - back[0:1])
             cd[h, 0:1, slot * ROWS : (slot + 1) * ROWS] = factor * back[1:2]
@@ -356,29 +345,29 @@
         for off in stage(route, n):
             slot = SLOT[off]
             src = dq_part.at[h, slot]
-            before = feeders(route, off)
-            if before:
+            if feeders(route, off):
                 total = dq_part[h, slot].astype(F32)
-                for o in before:
-                    total += dq_in[h, s_recv("dq", h, o, (dq_in,))].astype(F32)
+                for i in s_recv("dq", h, off, (dq_in,), route):
+                    total += dq_in[h, i].astype(F32)
                 dq_mid[h, slot] = total.astype(BF)
                 src = dq_mid.at[h, slot]
             s_send("dq", h, off, (src,), (dq_in,), route)
 
     def dq_finish(h):
         total = dq_part[h, 0].astype(F32)
-        for o in feeders(DQ_ROUTE[h], 0):
-            total += dq_in[h, s_recv("dq", h, o, (dq_in,))].astype(F32)
+        for i in s_recv("dq", h, 0, (dq_in,), DQ_ROUTE[h]):
+            total += dq_in[h, i].astype(F32)
         gq_ref[:, h * HDIM : (h + 1) * HDIM] = (total * SCALE).T.astype(BF)
 
     def keys_to_sibling(h):
-        send(dkv_scr.at[h, pl.ds(SECT // 2, SECT // 2)], r1_sec.at[h], ("r1s", h), to_ctx=sibling)
+        src = dkv_scr.at[h, pl.ds(SECT // 2, SECT // 2)]
+        send(src, r1_sec.at[h], "r1s", ("r1s", h), to_ctx=sibling)
         src = dkv_scr.at[h, pl.ds(SECT + HIST // 2, HIST // 2)]
-        send(src, r1_hist.at[h], ("r1h", h), to_ctx=sibling)
+        send(src, r1_hist.at[h], "r1h", ("r1h", h), to_ctx=sibling)
 
     def keys_along_y(h):
-        recv(r1_sec.at[h], ("r1s", h))
-        recv(r1_hist.at[h], ("r1h", h))
+        recv(r1_sec.at[h], "r1s", ("r1s", h))
+        recv(r1_hist.at[h], "r1h", ("r1h", h))
         for dy in (2, 1, 3, 0):
             there = (NY - dy) % NY
             for name, got, total, into, start, size in (
@@ -390,7 +379,7 @@
                 total[h, rows, :] = (own + got[h, rows, :].astype(F32)).astype(BF)
                 if dy:
                     src = total.at[h, pl.ds(dy * size, size)]
-                    send(src, into.at[h, there], (name, h, there), to_ctx=at_y(dy))
+                    send(src, into.at[h, there], name, (name, h), to_ctx=at_y(dy))
 
     def keys_finish(h):
         cols = slice(h * HDIM, (h + 1) * HDIM)
@@ -399,8 +388,8 @@
             ("r2h", t_hist, r2_hist, HCAP, ghk_ref, ghv_ref),
         ):
             value = total[h, 0:size, :].astype(F32)
+            recv(into.at[h, pl.ds(1, NY - 1)], name, (name, h))
             for dy in range(1, NY):
-                recv(into.at[h, dy], (name, h, dy))
                 value = value + into[h, dy].astype(F32)
             k_out[:, cols] = (value[:, 0:HDIM] * SCALE).astype(BF)
             v_out[:, cols] = value[:, HDIM : 2 * HDIM].astype(BF)
@@ -412,24 +401,22 @@
         for dx in (2, 1, 3):
             there = (NX - dx) % NX
             src = w_all.at[:, half(at_x(dx) * OCOLS)]
-            send(src, w_far.at[there, :, half(0)], ("w", there), to_head=at_x(dx))
+            send(src, w_far.at[there, :, half(0)], "w", ("w",), to_head=at_x(dx))
 
     def w_second():
-        for dx in (1, 3, 2):
-            recv(w_far.at[dx, :, half(0)], ("w", dx))
-            send(w_far.at[dx, :, half(0)], w_far.at[dx, :, half(0)], ("ws", dx), to_ctx=sibling)
+        recv(w_far.at[pl.ds(1, NX - 1), :, half(0)], "w", ("w",))
+        part = w_far.at[pl.ds(1, NX - 1), :, half(0)]
+        send(part, part, "ws", ("ws",), to_ctx=sibling)
 
     def w_rest():
-        for dx in (1, 3, 2):
-            recv(w_far.at[dx, :, half(0)], ("ws", dx))
+        recv(w_far.at[pl.ds(1, NX - 1), :, half(0)], "ws", ("ws",))
 
     def project(heads, first, last):
         rows = slice(heads[0] * HDIM, (heads[-1] + 1) * HDIM)
         total = None if first else acc[...]
+        for h in heads:
+            recv(at_all.at[h, pl.ds(1, NX - 1)], "at", ("at", h))
         for dx in (0, 1, 3, 2):
-            if dx:
-                for h in heads:
-                    recv(at_all.at[h, dx], ("at", h, dx))
             left = jnp.concatenate([at_all[h, dx] for h in heads], axis=1)
             part = dot_nn(left, w_far[dx, rows, :] if dx else w_cols(0)[rows, :])
             total = part if total is None else total + part
@@ -525,9 +512,28 @@
     keys_finish(2)
     dq_finish(2)
 
-    for copy in sent:
-        copy.wait_send()
-    assert len(sems.names) <= N_SEMS, len(sems.names)
+    seven = pl.ds(0, NZ - 1)
+    for group, same_size in {
+        "q": q_all.at[:, pl.ds(0, (NZ - 1) * ROWS), :],
+        "d": do_all.at[:, pl.ds(0, (NZ - 1) * ROWS), :],
+        "kv": kv_all.at[:, :, pl.ds(0, (NY - 1) * (ROWS + HCAP)), :],
+        "kvs": kv_all.at[:, :, pl.ds(0, NY * (ROWS + HCAP)), :],
+        "g": g_all.at[pl.ds(0, NX - 1)],
+        "w": w_far.at[pl.ds(0, NX - 1), :, half(0)],
+        "ws": w_far.at[pl.ds(0, NX - 1), :, half(0)],
+        ("o", 0): o_in.at[:, seven],
+        ("o", 1): st_in.at[:, seven],
+        "ret": ret_recv.at[:, seven],
+        "at": at_all.at[:, pl.ds(0, NX - 1)],
+        ("dq", 0): dq_in.at[:, seven],
+        "r1s": r1_sec,
+        "r1h": r1_hist,
+        "r2s": r2_sec.at[:, pl.ds(0, NY - 1)],
+        "r2h": r2_hist.at[:, pl.ds(0, NY - 1)],
+    }.items():
+        remote(same_size, same_size, group, ("w",), sibling, None).wait_send()
+    assert len(groups.names) <= N_SEND, len(groups.names)
+    assert len(arrivals.names) <= N_RECV, len(arrivals.names)
 
 
 def write_kernel(*refs):
@@ -591,8 +597,8 @@
         pltpu.VMEM((HEADS, NX, ROWS, HDIM), BF),
         pltpu.VMEM((NX, WIDTH, OCOLS), BF),
         pltpu.VMEM((ROWS, OCOLS), F32),
-        pltpu.SemaphoreType.DMA((N_SEMS,)),
-        pltpu.SemaphoreType.DMA((N_SEMS,)),
+        pltpu.SemaphoreType.DMA((N_SEND,)),
+        pltpu.SemaphoreType.DMA((N_RECV,)),
         pltpu.SemaphoreType.DMA(()),
     ]
     shapes = [

time: 69.3 us -> 65.6 us (0.947)
  Pallas kernels: 68.4 us -> 64.7 us
    pallas_call x1, Pallas kernels: 66.5 us -> 62.8 us  [shards(): pl.pallas_call(kernel, out_shape=shapes, in_specs=[vmem] * 5 + [smem] * 2...]
where the time goes in v4:
time: 65.6 us; the launch traced here: 65.5 us
  Pallas kernels  64.7 us (99%)
  between operations  0.8 us (1%)
    pallas_call x1, Pallas kernels, shards(): pl.pallas_call(kernel, out_shape=shapes, in_specs=[vmem] * 5 + [smem] * 2...  62.8 us
    pallas_call x1, Pallas kernels, write(): pl.pallas_call(write_kernel, out_shape=[jax.ShapeDtypeStruct(a.shape, a.d...  1.92 us

profile of v4, /device:TPU:1, one launch (start us, length us, event | category | flops | bytes accessed | tf_op | source)
XLA Modules:
  0.0 65.5 jit_solution(6650077130772856499)
XLA Ops:
  0.6 62.8 %shard_map.136 = (bf16[128,768]{1,0:T(8,128)(2,1)}, bf16[128,384]{1,0:T(8,128)(2,1)}, bf16[128,384]{1,0:T(8,128)(2,1)}, bf16[128,384]{1,0:T(8,128)(2,1)}, bf16[3...) custom-call(bf16[128,384]{1,0:T(8,128)(2,1)} %q_ref.1, bf16[128,384]{1,0:T(8,128)(2,1)} %k_ref.1, bf16[128,384]{1,0:T(8,128)(2,1)} %v_ref.1, ...), custom_call_target="tpu_custom_call" | custom-call | tf_op jit(solution)/shard_map/pallas_call | solution.py:612
  63.4 1.9 %shard_map.137 = (bf16[128,768]{1,0:T(8,128)(2,1)}, bf16[128,384]{1,0:T(8,128)(2,1)}, bf16[128,384]{1,0:T(8,128)(2,1)}, bf16[128,384]{1,0:T(8,128)(2,1)}, bf16[3...) custom-call(bf16[128,768]{1,0:T(8,128)(2,1)} %get-tuple-element.12.refs_0_, bf16[128,384]{1,0:T(8,128)(2,1)} %get-tuple-element.13.refs_1_, ...), custom_call_target="tpu_custom_call" | custom-call | tf_op jit(solution)/shard_map/pallas_call | solution.py:551

commit v5 on v4

--- a/solution.py
+++ b/solution.py
@@ -71,7 +71,7 @@
         return self.names.setdefault(name, len(self.names))
 
 
-N_SEND, N_RECV = 16, 88
+N_SEND, N_RECV = 16, 78
 Q_ROUTE, D_ROUTE = TWO, THREE
 O_ROUTE = (TWO, TWO, TWO)
 DQ_ROUTE = (DIRECT, TWO, TWO)
@@ -325,18 +325,18 @@
                 cols = slice(pair * CHUNK, (pair + 1) * CHUNK)
                 dp = dot_nt(value, dop[h, cols, :])
                 ds = p_scr[h, rows, cols].astype(F32) * (dp - cd[h, 0:1, cols])
-                ds_scr[rows, cols] = ds.astype(BF)
+                ds_scr[h % 2, rows, cols] = ds.astype(BF)
 
     def keys_back(h, chunks):
         for c in chunks:
             rows = slice(c * CHUNK, (c + 1) * CHUNK)
-            dkv_scr[h, rows, 0:HDIM] = dot_nn(ds_scr[rows, :], q_all[h]).astype(BF)
+            dkv_scr[h, rows, 0:HDIM] = dot_nn(ds_scr[h % 2, rows, :], q_all[h]).astype(BF)
             dkv_scr[h, rows, HDIM : 2 * HDIM] = dot_nn(p_scr[h, rows, :], dop[h]).astype(BF)
 
     def queries_back(h):
         for pair in (3, 2, 1, 0):
             cols = slice(pair * CHUNK, (pair + 1) * CHUNK)
-            dq = dot_nn(kt[h], ds_scr[:, cols])
+            dq = dot_nn(kt[h], ds_scr[h % 2, :, cols])
             for i in range(2):
                 dq_part[h, 2 * pair + i] = dq[:, i * ROWS : (i + 1) * ROWS].astype(BF)
 
@@ -575,7 +575,7 @@
         pltpu.VMEM((KT, CHUNK), F32),
         pltpu.VMEM((HEADS, KT, QT), BF),
         pltpu.VMEM(box, BF),
-        pltpu.VMEM((KT, QT), BF),
+        pltpu.VMEM((2, KT, QT), BF),
         pltpu.VMEM(box, BF),
         pltpu.VMEM((HEADS, KT, 2 * HDIM), BF),
         pltpu.VMEM((HEADS, NZ, 2, ROWS), F32),

time: 65.6 us -> 65.5 us (level)
  no operation moved by 1% of the time
where the time goes in v5:
time: 65.5 us; the launch traced here: 65.4 us
  Pallas kernels  64.6 us (99%)
  between operations  0.8 us (1%)
    pallas_call x1, Pallas kernels, shards(): pl.pallas_call(kernel, out_shape=shapes, in_specs=[vmem] * 5 + [smem] * 2...  62.7 us
    pallas_call x1, Pallas kernels, write(): pl.pallas_call(write_kernel, out_shape=[jax.ShapeDtypeStruct(a.shape, a.d...  1.92 us

profile of v5, /device:TPU:1, one launch (start us, length us, event | category | flops | bytes accessed | tf_op | source)
XLA Modules:
  0.0 65.4 jit_solution(8859736815200099599)
XLA Ops:
  0.6 62.7 %shard_map.136 = (bf16[128,768]{1,0:T(8,128)(2,1)}, bf16[128,384]{1,0:T(8,128)(2,1)}, bf16[128,384]{1,0:T(8,128)(2,1)}, bf16[128,384]{1,0:T(8,128)(2,1)}, bf16[3...) custom-call(bf16[128,384]{1,0:T(8,128)(2,1)} %q_ref.1, bf16[128,384]{1,0:T(8,128)(2,1)} %k_ref.1, bf16[128,384]{1,0:T(8,128)(2,1)} %v_ref.1, ...), custom_call_target="tpu_custom_call" | custom-call | tf_op jit(solution)/shard_map/pallas_call | solution.py:612
  63.3 1.9 %shard_map.137 = (bf16[128,768]{1,0:T(8,128)(2,1)}, bf16[128,384]{1,0:T(8,128)(2,1)}, bf16[128,384]{1,0:T(8,128)(2,1)}, bf16[128,384]{1,0:T(8,128)(2,1)}, bf16[3...) custom-call(bf16[128,768]{1,0:T(8,128)(2,1)} %get-tuple-element.12.refs_0_, bf16[128,384]{1,0:T(8,128)(2,1)} %get-tuple-element.13.refs_1_, ...), custom_call_target="tpu_custom_call" | custom-call | tf_op jit(solution)/shard_map/pallas_call | solution.py:551
